TPU v7x, 32 devices: a whole 2x2x4 slice. The times are simulated.
32 devices in a mesh: seq: 4 (over x, core), batch: 2 (over y), tensor: 4 (over z).
Axes of the slice: x: 2, y: 2, z: 4, core: 2. Of those that a mesh axis runs over, the one named last changes fastest.
Arguments:
- tokens: bfloat16 [8, 1024, 2048], P('batch', 'seq'), may hold values from -6 to 6
- cotangent: bfloat16 [8, 1024, 2048], P('batch', 'seq'), may hold values from -6 to 6
- lengths: int32 [8], P('batch'), may hold values from 512 to 1024, as said below
- block_slot: int32 [4], replicated, may hold values from 0 to 3, each once
- gain_attn: float32 [2048], replicated, may hold values from 0.5 to 1.5
- shift_attn: float32 [2048], replicated, may hold values from -1.75 to 1.75
- gain_mlp: float32 [2048], replicated, may hold values from 0.5 to 1.5
- shift_mlp: float32 [2048], replicated, may hold values from -1.75 to 1.75
- w_qkv: bfloat16 [2048, 8, 768], P(('seq', 'batch'), 'tensor'), may hold values from -0.125 to 0.125
- b_qkv: float32 [8, 768], P('tensor'), may hold values from -1.75 to 1.75
- w_out: bfloat16 [2048, 2048], P('tensor', ('seq', 'batch')), may hold values from -2 to 2
- b_out: float32 [2048], replicated, may hold values from -1.75 to 1.75
- w_up: bfloat16 [2048, 8192], P(('seq', 'batch'), 'tensor'), may hold values from -0.125 to 0.125
- b_up: float32 [8192], P('tensor'), may hold values from -1.75 to 1.75
- w_down: bfloat16 [8192, 2048], P('tensor', ('seq', 'batch')), may hold values from -0.0625 to 0.0625
- b_down: float32 [2048], replicated, may hold values from -1.75 to 1.75
Outputs:
- mixed: bfloat16 [8, 1024, 2048], P('batch', 'seq')
- tokens_grad: float32 [8, 1024, 2048], P('batch', 'seq')
- gain_attn_grad: float32 [2048], replicated
- shift_attn_grad: float32 [2048], replicated
- gain_mlp_grad: float32 [2048], replicated
- shift_mlp_grad: float32 [2048], replicated
- w_qkv_grad: float32 [2048, 8, 768], P(('seq', 'batch'), 'tensor')
- b_qkv_grad: float32 [8, 768], P('tensor')
- w_out_grad: float32 [2048, 2048], P('tensor', ('seq', 'batch'))
- b_out_grad: float32 [2048], replicated
- w_up_grad: float32 [2048, 8192], P(('seq', 'batch'), 'tensor')
- b_up_grad: float32 [8192], P('tensor')
- w_down_grad: float32 [8192, 2048], P('tensor', ('seq', 'batch'))
- b_down_grad: float32 [2048], replicated
Inputs may be any that keep to these rules, and one draw needn't show every extreme that they name: `lengths`: in every aligned block of 1 sequence one has length 1024. `block_slot`: every block index appears exactly once.
All inputs are finite; a program needn't handle non-finite values.
Results may differ from a plain program's by a relative error of at most 0.019.
Values may be sent and summed in bfloat16 or wider, within the bound.
No kernel may reach another device: no remote copies, remote signals or barrier semaphores. Data moves between devices by JAX's collectives and lax.ppermute only.
A program may use at most 192 MiB of HBM per device.

v0:
```python
import jax
import jax.numpy as jnp
from jax import lax
from jax.experimental import pallas as pl
from jax.experimental.pallas import tpu as pltpu
from jax.sharding import PartitionSpec as P

D = 2048
HEAD_DIM = 256
ROT = 64
EPS = 1e-05
FLOOR = -1e30
BF = jnp.bfloat16
F32 = jnp.float32


def dot(a, b, dims):
    return lax.dot_general(a, b, (dims, ((), ())), preferred_element_type=F32)


def rotation(places):
    half_rot = ROT // 2
    frequency = 10000.0 ** (jnp.arange(half_rot, dtype=F32) * (-2.0 / ROT))
    angles = places.astype(F32)[:, None] * frequency[None, :]
    return jnp.cos(angles)[:, None, :], jnp.sin(angles)[:, None, :]


def rotate(field, cosine, sine):
    half_rot = ROT // 2
    front = field[..., :half_rot]
    back = field[..., half_rot:ROT]
    return jnp.concatenate(
        [front * cosine - back * sine, back * cosine + front * sine, field[..., ROT:]], -1
    )


def gelu_pair(z):
    phi_cdf = 0.5 * (1.0 + lax.erf(z * 0.7071067811865476))
    density = 0.3989422804014327 * jnp.exp(-0.5 * z * z)
    return z * phi_cdf, phi_cdf + z * density


def per_device_any(
    tokens,
    cotangent,
    lengths,
    block_slot,
    gain_attn,
    shift_attn,
    gain_mlp,
    shift_mlp,
    w_qkv,
    b_qkv,
    w_out,
    b_out,
    w_up,
    b_up,
    w_down,
    b_down,
):
    seqs, block_rows, _ = tokens.shape
    rows = seqs * block_rows
    shard = w_qkv.shape[0]
    heads = w_qkv.shape[1]
    width_qkv = heads * 3 * HEAD_DIM
    width_att = heads * HEAD_DIM
    units = w_up.shape[1]
    fsdp = ("seq", "batch")
    scale = HEAD_DIM ** (-0.5)
    seq_count = lax.axis_size("seq")
    device_ids = jnp.arange(seq_count, dtype=jnp.int32)
    own_slot = jnp.sum(jnp.where(device_ids == lax.axis_index("seq"), block_slot, 0))
    offsets = jnp.arange(block_rows, dtype=jnp.int32)
    query_places = own_slot * block_rows + offsets
    key_places = (block_slot[:, None] * block_rows + offsets[None, :]).reshape(-1)

    attn_shard = jnp.concatenate([w_qkv.reshape(shard, width_qkv), w_out.T], 1)
    mlp_shard = jnp.concatenate([w_up, w_down.T], 1)
    attn_full = lax.all_gather(attn_shard, fsdp, axis=0, tiled=True)
    mlp_full = lax.all_gather(mlp_shard, fsdp, axis=0, tiled=True)
    full_qkv = attn_full[:, :width_qkv]
    full_out_t = attn_full[:, width_qkv:]
    full_up = mlp_full[:, :units]
    full_down_t = mlp_full[:, units:]

    token_rows = tokens.astype(F32).reshape(rows, D)
    centered = token_rows - jnp.mean(token_rows, -1, keepdims=True)
    inverse = lax.rsqrt(jnp.mean(jnp.square(centered), -1, keepdims=True) + EPS)
    xhat = centered * inverse
    input_attn = (xhat * gain_attn + shift_attn).astype(BF)
    input_mlp = (xhat * gain_mlp + shift_mlp).astype(BF)

    valid = (query_places[None, :] < lengths[:, None]).astype(F32)
    grad_rows = (cotangent.astype(F32) * valid[..., None]).reshape(rows, D)
    grad_low = grad_rows.astype(BF)

    project = dot(input_attn, full_qkv, ((1,), (0,))).reshape(
        seqs, block_rows, heads, 3 * HEAD_DIM
    ) + b_qkv
    cosine, sine = rotation(query_places)
    queries = rotate(project[..., :HEAD_DIM], cosine, sine).astype(BF)
    keys = rotate(project[..., HEAD_DIM : 2 * HEAD_DIM], cosine, sine).astype(BF)
    values = project[..., 2 * HEAD_DIM :].astype(BF)
    pair = jnp.concatenate([keys, values], -1)
    gathered = lax.all_gather(pair, "seq", axis=0, tiled=False)
    gathered = jnp.transpose(gathered, (1, 3, 0, 2, 4)).reshape(
        seqs, heads, seq_count * block_rows, 2 * HEAD_DIM
    )
    all_keys = gathered[..., :HEAD_DIM]
    all_values = gathered[..., HEAD_DIM:]

    hidden_pre = dot(input_mlp, full_up, ((1,), (0,))) + b_up
    gelu, slope = gelu_pair(hidden_pre)
    activated = gelu.astype(BF)
    grad_hidden = dot(grad_low, full_down_t, ((1,), (0,))) * slope
    hidden_low = grad_hidden.astype(BF)
    bias_up_sum = jnp.sum(grad_hidden, 0)

    grad_att = dot(grad_low, full_out_t, ((1,), (0,))).reshape(
        seqs, block_rows, heads, HEAD_DIM
    ).astype(BF)

    causal = key_places[None, None, :] <= query_places[None, :, None]
    inside = key_places[None, None, :] < lengths[:, None, None]
    mask = (causal & inside)[:, None]
    scores = jnp.einsum("schd,shtd->shct", queries, all_keys, preferred_element_type=F32) * scale
    scores = jnp.where(mask, scores, FLOOR)
    top = jnp.max(scores, -1, keepdims=True)
    weights = jnp.where(mask, jnp.exp(scores - top), 0.0)
    probs = weights / jnp.sum(weights, -1, keepdims=True)
    prob_low = probs.astype(BF)
    attended = jnp.einsum("shct,shtd->schd", prob_low, all_values, preferred_element_type=F32)
    attended = attended.astype(BF).reshape(rows, width_att)

    partial = dot(attended, full_out_t, ((1,), (1,))) + dot(activated, full_down_t, ((1,), (1,)))
    branch = lax.psum(partial.astype(BF), "tensor").astype(F32)

    grad_mlp_weights = jnp.concatenate(
        [dot(input_mlp, hidden_low, ((0,), (0,))), dot(grad_low, activated, ((0,), (0,)))], 1
    ).astype(BF)
    mlp_reduced = lax.psum_scatter(
        grad_mlp_weights, fsdp, scatter_dimension=0, tiled=True
    ).astype(F32)

    grad_probs = jnp.einsum("schd,shtd->shct", grad_att, all_values, preferred_element_type=F32)
    delta = jnp.sum(probs * grad_probs, -1, keepdims=True)
    grad_scores = (probs * (grad_probs - delta)).astype(BF)
    grad_query = jnp.einsum("shct,shtd->schd", grad_scores, all_keys, preferred_element_type=F32) * scale
    key_term = jnp.einsum("shct,schd->tshd", grad_scores, queries, preferred_element_type=F32) * scale
    value_term = jnp.einsum("shct,schd->tshd", prob_low, grad_att, preferred_element_type=F32)
    terms = jnp.concatenate([key_term, value_term], -1).astype(BF)
    own_terms = lax.psum_scatter(terms, "seq", scatter_dimension=0, tiled=True).astype(F32)
    own_terms = jnp.swapaxes(own_terms, 0, 1)
    grad_key = own_terms[..., :HEAD_DIM]
    grad_value = own_terms[..., HEAD_DIM:]
    grad_project = jnp.concatenate(
        [rotate(grad_query, cosine, -sine), rotate(grad_key, cosine, -sine), grad_value], -1
    ).reshape(rows, width_qkv)
    bias_qkv_sum = jnp.sum(grad_project, 0)
    project_low = grad_project.astype(BF)

    grad_norm_attn = dot(project_low, full_qkv, ((1,), (1,)))
    grad_norm_mlp = dot(hidden_low, full_up, ((1,), (1,)))
    norm_sums = jnp.stack(
        [
            jnp.sum(grad_norm_attn * xhat, 0),
            jnp.sum(grad_norm_attn, 0),
            jnp.sum(grad_norm_mlp * xhat, 0),
            jnp.sum(grad_norm_mlp, 0),
        ]
    )
    grad_xhat = grad_norm_attn * gain_attn + grad_norm_mlp * gain_mlp
    input_part = inverse * (
        grad_xhat
        - jnp.mean(grad_xhat, -1, keepdims=True)
        - xhat * jnp.mean(grad_xhat * xhat, -1, keepdims=True)
    )
    input_part, branch = lax.optimization_barrier((input_part.astype(BF), branch))
    input_sum = lax.psum(input_part, "tensor").astype(F32)
    mixed = (token_rows + branch + b_out + b_down).astype(BF).reshape(tokens.shape)
    tokens_grad = (grad_rows + input_sum).reshape(tokens.shape)

    grad_attn_weights = jnp.concatenate(
        [dot(input_attn, project_low, ((0,), (0,))), dot(grad_low, attended, ((0,), (0,)))], 1
    ).astype(BF)
    attn_reduced = lax.psum_scatter(
        grad_attn_weights, fsdp, scatter_dimension=0, tiled=True
    ).astype(F32)

    norm_sums = lax.psum(norm_sums, "tensor").reshape(-1)
    small = lax.psum(
        jnp.concatenate([norm_sums, bias_qkv_sum, jnp.sum(grad_rows, 0), bias_up_sum]), fsdp
    )
    norm_sums = small[: 4 * D].reshape(4, D)
    small = small[4 * D :]
    bias_qkv_sum = small[:width_qkv].reshape(b_qkv.shape)
    bias_out_sum = small[width_qkv : width_qkv + D]
    bias_up_sum = small[width_qkv + D :]
    return (
        mixed,
        tokens_grad,
        norm_sums[0],
        norm_sums[1],
        norm_sums[2],
        norm_sums[3],
        attn_reduced[:, :width_qkv].reshape(w_qkv.shape),
        bias_qkv_sum,
        attn_reduced[:, width_qkv:].T,
        bias_out_sum,
        mlp_reduced[:, :units],
        bias_up_sum,
        mlp_reduced[:, units:].T,
        bias_out_sum,
    )


def exchange(array, axis, flip):
    size = lax.axis_size(axis)
    return lax.ppermute(array, axis, [(i, i ^ flip) for i in range(size)])


def after(array, *others):
    return lax.optimization_barrier((array, *others))[0]


def along_x(array):
    return exchange(array, "seq", 2)


def along_y(array):
    return exchange(array, "batch", 1)


def to_core(array):
    return exchange(array, "seq", 1)


ORDER = (0, 2, 4, 6, 1, 3, 5, 7)


def block_ins(blocks, width, column):
    return [(pl.BlockSpec((256, width), lambda j: (0, column(j))), b) for b in blocks]


def both_cores(own, by_x, by_y, far, *others):
    own_c, by_x_c, by_y_c, far_c = others
    return (own, by_y, own_c, by_y_c, by_x, far, by_x_c, far_c)


def call(body, grid, ins, outs, scratch=(), flops=0, moved=0, vmem=60, aliases={}):
    return pl.pallas_call(
        body,
        grid=grid,
        in_specs=[spec for spec, _ in ins],
        out_specs=[spec for spec, _ in outs],
        out_shape=[shape for _, shape in outs],
        scratch_shapes=list(scratch),
        input_output_aliases=aliases,
        compiler_params=pltpu.CompilerParams(vmem_limit_bytes=vmem * 1024 * 1024),
        cost_estimate=pl.CostEstimate(flops=0, bytes_accessed=0, transcendentals=0),
    )(*[array for _, array in ins])


def call_placed(body, grid, info, ins, outs, scratch=(), flops=0, moved=0, vmem=60):
    return pl.pallas_call(
        body,
        grid_spec=pltpu.PrefetchScalarGridSpec(
            num_scalar_prefetch=1,
            grid=grid,
            in_specs=[spec for spec, _ in ins],
            out_specs=[spec for spec, _ in outs],
            scratch_shapes=list(scratch),
        ),
        out_shape=[shape for _, shape in outs],
        compiler_params=pltpu.CompilerParams(vmem_limit_bytes=vmem * 1024 * 1024),
        cost_estimate=pl.CostEstimate(flops=0, bytes_accessed=0, transcendentals=0),
    )(info, *[array for _, array in ins])


def smem():
    return pl.BlockSpec(memory_space=pltpu.SMEM)


def any_place():
    return pl.BlockSpec(memory_space=pl.ANY)


def whole(array):
    dims = len(array.shape)
    return pl.BlockSpec(array.shape, lambda *_: (0,) * dims, pipeline_mode=pl.Buffered(1))


def block(shape, index):
    return pl.BlockSpec(shape, index)


def struct(shape, dtype):
    return jax.ShapeDtypeStruct(shape, dtype)


def columns(ref, info, place):
    start = pl.multiple_of((info[0] ^ place) * 256, 256)
    return ref[:, pl.ds(start, 256)]


def norm_body(info, tok, cot, gain_a, shift_a, gain_m, shift_m, in_a, in_m, grad, grad_sum):
    step = pl.program_id(0)
    t = tok[...].astype(F32)
    centered = t - jnp.mean(t, -1, keepdims=True)
    xhat = centered * lax.rsqrt(jnp.mean(centered * centered, -1, keepdims=True) + EPS)
    in_a[...] = (xhat * gain_a[...] + shift_a[...]).astype(BF)
    in_m[...] = (xhat * gain_m[...] + shift_m[...]).astype(BF)
    place = info[1] * 256 + lax.broadcasted_iota(jnp.int32, t.shape, 0)
    g = jnp.where(place < info[5 + step], cot[...].astype(F32), 0.0)
    grad[...] = g.astype(BF)

    @pl.when(step == 0)
    def _():
        grad_sum[...] = jnp.zeros_like(grad_sum)

    grad_sum[...] += jnp.sum(g, 0, keepdims=True)


def matched(x, blocks, info):
    left = jnp.concatenate([columns(x, info, r) for r in range(8)], 1)
    right = jnp.concatenate([b[...] for b in blocks], 0)
    return jnp.dot(left, right, preferred_element_type=F32)


def turn(z, cos, front, back):
    first = z[:, :128]
    first = (
        first * cos
        + pltpu.roll(first, 96, 1) * front
        + pltpu.roll(first, 32, 1) * back
    )
    return jnp.concatenate([first, z[:, 128:]], 1)


def qkv_body(info, x, bias, cos, front, back, *refs):
    blocks, (q, kv_a, kv_b) = (refs[:8], refs[8:16]), refs[16:]
    step = pl.program_id(0)
    heads = [matched(x, blocks[h], info) + bias[h : h + 1] for h in range(2)]

    def turned():
        c, f, b = (jnp.concatenate([t[...]] * 4, 0) for t in (cos, front, back))
        return jnp.concatenate([turn(z, c, f, b) for z in heads], 1).astype(BF)

    @pl.when(step == 0)
    def _():
        q[...] = turned()

    @pl.when(step == 1)
    def _():
        k = turned()
        kv_a[...] = k[:512]
        kv_b[...] = k[512:]

    @pl.when(step == 2)
    def _():
        v = jnp.concatenate(heads, 1).astype(BF)
        kv_a[...] = v[:512]
        kv_b[...] = v[512:]


def split_body(from_x, from_y, top, bottom):
    top[...] = from_x[...]
    bottom[...] = from_y[...]


def grad_att_body(info, g, *refs):
    refs[16][...] = jnp.concatenate(
        [matched(g, refs[:8], info), matched(g, refs[8:16], info)], 1
    ).astype(BF)


def up_body(info, x, bias, *refs):
    blocks, (act, slope) = refs[:8], refs[8:]
    z = matched(x, blocks, info) + bias[...]
    gelu, steep = gelu_pair(z)
    act[...] = gelu.astype(BF)
    slope[...] = steep.astype(BF)


def hidden_body(info, g, slope, *refs):
    low, total = refs[8:]
    grad = matched(g, refs[:8], info) * slope[...].astype(F32)
    low[...] = grad.astype(BF)
    total[...] = jnp.sum(grad, 0, keepdims=True)


def nt(a, b):
    return lax.dot_general(a, b, (((1,), (1,)), ((), ())), preferred_element_type=F32)


def tn(a, b):
    return lax.dot_general(a, b, (((0,), (0,)), ((), ())), preferred_element_type=F32)


def attention_body(first_seq, info, q_ref, ga_ref, cos, front, back, *refs):
    keys, values = refs[:4], refs[4:8]
    att, dq, dq_sum, keep, send = refs[8:]
    terms = (keep.at[0], send.at[0], keep.at[1], send.at[1])
    seq = pl.program_id(0)
    head = pl.program_id(1)
    scale = HEAD_DIM ** (-0.5)
    length = info[5 + first_seq + seq]
    q = q_ref[...] * jnp.asarray(scale, BF)
    ga = ga_ref[...]
    last_seen = jnp.minimum(
        info[1] * 256 + lax.broadcasted_iota(jnp.int32, (256, 256), 0), length - 1
    )
    column = lax.broadcasted_iota(jnp.int32, (256, 256), 1)
    scores = [
        jnp.where(info[1 + r] * 256 + column <= last_seen, nt(q, keys[r][...]), FLOOR) for r in range(4)
    ]
    top = jnp.max(jnp.maximum(jnp.maximum(scores[0], scores[1]), jnp.maximum(scores[2], scores[3])), -1, keepdims=True)
    weights = [jnp.exp(s - top) for s in scores]
    total = jnp.sum(weights[0] + weights[1] + weights[2] + weights[3], -1, keepdims=True)
    inverse = 1.0 / total
    probs = [w * inverse for w in weights]
    low = [p.astype(BF) for p in probs]
    out = jnp.zeros((256, 256), F32)
    for r in range(4):
        out += jnp.dot(low[r], values[r][...], preferred_element_type=F32)
    att[...] = out.astype(BF)
    grad_probs = [nt(ga, values[r][...]) for r in range(4)]
    products = [p * g for p, g in zip(probs, grad_probs)]
    delta = jnp.sum(products[0] + products[1] + products[2] + products[3], -1, keepdims=True)
    grad_q = jnp.zeros((256, 256), F32)
    key_columns = pl.ds(pl.multiple_of(head * 256, 256), 256)
    value_columns = pl.ds(pl.multiple_of(head * 256 + 512, 256), 256)
    for r in range(4):
        grad_scores = (probs[r] * (grad_probs[r] - delta)).astype(BF)
        grad_q += jnp.dot(grad_scores, keys[r][...], preferred_element_type=F32)
        terms[r][:, key_columns] = tn(grad_scores, q).astype(BF)
        terms[r][:, value_columns] = tn(low[r], ga).astype(BF)
    grad_q = turn(grad_q * scale, cos[...], -front[...], -back[...])
    dq[...] = grad_q.astype(BF)
    dq_sum[...] = jnp.sum(grad_q, 0, keepdims=True)[None, None]


def streamed(blocks, width, column):
    return [(pl.BlockSpec((256, width), lambda i: (0, column(i))), blocks[r]) for r in ORDER]


def branch_body(info, att, act, *refs):
    w_att, w_act, outs, total = refs[:8], refs[8:16], refs[16:18], refs[18]
    step = pl.program_id(0)

    def part(i):
        return nt(att[...], w_att[i][...]) + nt(act[...], w_act[i][...])

    @pl.when(step == 0)
    def _():
        for i in range(8):
            total[:, i * 256 : (i + 1) * 256] = part(i)

    @pl.when(step == 1)
    def _():
        for i, r in enumerate(ORDER):
            there = pl.ds(pl.multiple_of((info[0] ^ r) * 256, 256), 256)
            done = (total[:, i * 256 : (i + 1) * 256] + part(i)).astype(BF)
            outs[0][:, there] = done[:256]
            outs[1][:, there] = done[256:]


def weight_part(refs):
    products = [tn(refs[i][...], refs[i + 1][...]) for i in range(0, len(refs), 2)]
    return products[0] if len(products) == 1 else jnp.concatenate(products, 1)


def weight_send_body(info, *refs):
    refs[-1][...] = weight_part(refs[:-1]).astype(BF)


def weight_add_body(info, *refs):
    received, over_x, over_y, next_y, next_x, own = refs[-6:]
    step = pl.program_id(0)
    part = (weight_part(refs[:-6]) + received[...].astype(F32)).astype(BF)
    left, right = part[:, :1024], part[:, 1024:]

    @pl.when(step == 0)
    def _():
        over_x[...] = left
        next_x[...] = right

    @pl.when(step == 1)
    def _():
        over_x[...] = left
        over_y[...] = right

    @pl.when(step == 2)
    def _():
        next_y[...] = left
        over_y[...] = right

    @pl.when(step == 3)
    def _():
        own[...] = part


class Scatter:
    def __init__(self, pairs):
        self.pairs = pairs

    def operands(self, flip):
        def index(i, info):
            place = jnp.where(i == 0, 4, jnp.where(i == 1, 5, jnp.where(i == 2, 1, 0)))
            return 0, info[0] ^ place ^ flip

        fixed = lambda array: pl.BlockSpec(array.shape, lambda i, info: (0, 0), pipeline_mode=pl.Buffered(1))
        return [
            operand
            for x, h in self.pairs
            for operand in ((block((1024, 256), index), x), (fixed(h), h))
        ]

    def send(self, info):
        self.sent = call_placed(
            weight_send_body,
            (4,),
            info,
            self.operands(2),
            [(block((256, 2048), lambda i, info: (i, 0)), struct((1024, 2048), BF))],
        )[0]
        return self.sent

    def add(self, info, received):
        clip = lambda first: lambda i, info: (jnp.clip(i - first, 0, 1), 0)
        fixed = lambda width: (block((256, width), lambda i, info: (0, 0)), struct((256, width), BF))
        tall = lambda first: (block((256, 1024), clip(first)), struct((512, 1024), BF))
        made = call_placed(
            weight_add_body,
            (4,),
            info,
            self.operands(0) + [(block((256, 2048), lambda i, info: (i, 0)), received)],
            [tall(0), tall(1), fixed(1024), fixed(1024), fixed(2048)],
        )
        self.over_x, self.over_y, self.next_y, self.next_x, self.own = made
        return self.own

    def first(self, done):
        self.from_x = along_x(after(self.over_x, done))
        self.from_y = along_y(after(self.over_y, done))
        return self.from_x, self.from_y

    def second(self, done):
        self.last_y = along_y(plus(after(self.next_y, done), self.from_x[256:]))
        self.last_x = along_x(plus(after(self.next_x, done), self.from_y[:256]))
        return self.last_y, self.last_x

    def total(self, info, turned=False):
        tall = lambda array, row: (block((256, 1024), lambda i: (row, 0)), array)
        shape = (2048, 256) if turned else (256, 2048)
        return call(
            total_turned_body if turned else total_body,
            (1,),
            [
                (smem(), info),
                (whole(self.own), self.own),
                tall(self.from_x, 0),
                tall(self.last_y, 0),
                tall(self.from_y, 1),
                tall(self.last_x, 0),
            ],
            [(block(shape, lambda i: (0, 0)), struct(shape, F32))],
        )[0]


def total_of(own, from_x, last_y, from_y, last_x):
    left = from_x[...].astype(F32) + last_y[...].astype(F32)
    right = from_y[...].astype(F32) + last_x[...].astype(F32)
    return own[...].astype(F32) + jnp.concatenate([left, right], 1)


def total_body(info, *refs):
    refs[-1][...] = total_of(*refs[:-1])


def total_turned_body(info, *refs):
    refs[-1][...] = total_of(*refs[:-1]).T


def project_body(info, q, own, core, far, cos, front, back, low, kv_sum):
    c, f, b = (jnp.concatenate([t[...]] * 2, 0) for t in (cos, front, back))
    for head in range(2):
        mine = slice(head * 256, head * 256 + 256)
        low[:, head * 768 : head * 768 + 256] = q[:, mine]
        for kind in range(2):
            cut = slice(kind * 512 + head * 256, kind * 512 + head * 256 + 256)
            grad = own[:, cut].astype(F32) + core[:, cut].astype(F32) + far[:, cut].astype(F32)
            if kind == 0:
                grad = turn(grad, c, -f, -b)
            kv_sum[:, head * 512 + kind * 256 : head * 512 + kind * 256 + 256] = jnp.sum(grad, 0, keepdims=True)
            start = head * 768 + 256 + kind * 256
            low[:, start : start + 256] = grad.astype(BF)


def input_body(info, low, hid, tok, gain_a, gain_m, *refs):
    w_qkv, w_up, parts, sums, (gx, xh, inv) = refs[:8], refs[8:16], refs[16:18], refs[18], refs[19:]
    step = pl.program_id(0)

    def products(first):
        for i, r in enumerate(ORDER):
            there = pl.ds(pl.multiple_of((info[0] ^ r) * 256, 256), 256)
            from_attn = nt(low[...], w_qkv[i][:, :768])
            from_mlp = nt(hid[...], w_up[i][...])
            xhat = xh[:, there]
            columns_sums = [from_attn * xhat, from_attn, from_mlp * xhat, from_mlp]
            grad = from_attn * gain_a[:, there] + from_mlp * gain_m[:, there]
            for row, values in enumerate(columns_sums):
                added = jnp.sum(values, 0, keepdims=True)
                sums[row : row + 1, there] = added if first else sums[row : row + 1, there] + added
            gx[:, there] = grad if first else gx[:, there] + grad

    @pl.when(step == 0)
    def _():
        t = tok[...].astype(F32)
        centered = t - jnp.mean(t, -1, keepdims=True)
        inverse = lax.rsqrt(jnp.mean(centered * centered, -1, keepdims=True) + EPS)
        xh[...] = centered * inverse
        inv[...] = jnp.broadcast_to(inverse, inv.shape)
        products(True)

    @pl.when(step == 1)
    def _():
        products(False)
        grad = gx[...]
        xhat = xh[...]
        mean = jnp.mean(grad, -1, keepdims=True)
        along = jnp.mean(grad * xhat, -1, keepdims=True)
        out = (inv[:, :1] * (grad - mean - xhat * along)).astype(BF)
        parts[0][...] = out[:256]
        parts[1][...] = out[256:]


def plus(a, b):
    return (a.astype(F32) + b.astype(F32)).astype(BF)


def bar(*arrays):
    return lax.optimization_barrier(arrays)


def finish_body(info, own, from_x, last_y, from_y, last_x, qkv, out):
    total = total_of(own, from_x, last_y, from_y, last_x)
    for head in range(2):
        qkv[:, head, :] = total[:, head * 768 : head * 768 + 768]
    out[...] = total[:, 1536:].T


class Hops:
    def __init__(self, info, tok, grad, bias):
        self.info = info
        self.given = (tok, grad, bias)
        self.mine = {}
        self.ready = {}
        self.pair = None
        self.out = [None, None]

    def start(self, block):
        self.leaving = self.mine[0] = block
        return [exchange(block, "tensor", 1)]

    def land(self, j, arrived, next_block=None):
        half = lambda array: (block((128, D), lambda i: (i, 0)), array)
        fresh = (block((128, D), lambda i: (i, 0)), struct((256, D), BF))
        parts, ins, outs = [], [(smem(), self.info)], []
        if j >= 2:
            self.ready[j - 2] = (self.leaving, arrived[0])
        if j < 8:
            parts.append("pair")
            ins += [half(self.mine[j]), half(arrived[0])]
            outs.append(fresh)
        if 1 <= j <= 8:
            parts.append("sum" if next_block is None else "either")
            ins += [half(self.pair), half(arrived[1])]
            if next_block is not None:
                ins.append(half(next_block))
            outs.append(fresh)
        made = list(call(lambda *refs: land_body(parts, *refs), (2,), ins, outs))
        done = made[0]
        if next_block is not None:
            self.mine[j + 1] = next_block
        pair = made.pop(0) if j < 8 else None
        self.leaving = made.pop(0) if j else after(next_block, pair)
        flying = [exchange(self.leaving, "tensor", 1)]
        if pair is not None:
            self.pair = pair
            flying.append(lax.ppermute(pair, "tensor", [(1, 2), (2, 1)]))
        return flying, done

    def write(self, k, before):
        tok, grad, bias = self.given
        which, place = divmod(k, 4)
        half = lambda array: (block((128, D), lambda i: (i, 0)), array)
        kept = (block((128, D), lambda i: (2 * place + i, 0)), (tok, grad)[which])
        ins = [(smem(), after(self.info, before))] + [half(array) for array in self.ready[k]] + [kept]
        if not which:
            ins.append((whole(bias), bias))
        aliases = {}
        if self.out[which] is not None:
            aliases[len(ins)] = 0
            ins.append((any_place(), self.out[which]))
        made = call(
            (mixed_body, tokens_grad_body)[which],
            (2,),
            ins,
            [(kept[0], struct((1024, D), (BF, F32)[which]))],
            aliases=aliases,
        )[0]
        self.out[which] = made
        return made


def land_body(parts, info, *refs):
    refs = list(refs)
    outs = refs[-len(parts) :]
    for part, out in zip(parts, outs):
        a, b = refs.pop(0), refs.pop(0)
        summed = (a[...].astype(F32) + b[...].astype(F32)).astype(BF)
        out[...] = jnp.where(info[9] > 0, summed, refs.pop(0)[...]) if part == "either" else summed


def tokens_grad_body(info, total, came, grad, *refs):
    refs[-1][...] = jnp.where(info[9] > 0, total[...], came[...]).astype(F32) + grad[...].astype(F32)


def mixed_body(info, total, came, tok, bias, *refs):
    summed = jnp.where(info[9] > 0, total[...], came[...]).astype(F32) + tok[...].astype(F32)
    refs[-1][...] = (summed + bias[...]).astype(BF)


def per_device_links(
    tokens,
    cotangent,
    lengths,
    block_slot,
    gain_attn,
    shift_attn,
    gain_mlp,
    shift_mlp,
    w_qkv,
    b_qkv,
    w_out,
    b_out,
    w_up,
    b_up,
    w_down,
    b_down,
):
    rows = 1024
    seq_id = lax.axis_index("seq")
    slots = [jnp.sum(jnp.where(jnp.arange(4) == (seq_id ^ r), block_slot, 0)) for r in range(4)]
    tensor_id = lax.axis_index("tensor")
    inner = ((tensor_id == 1) | (tensor_id == 2)).astype(jnp.int32)
    me = seq_id * 2 + lax.axis_index("batch")
    info = jnp.concatenate([jnp.stack([me, *slots]), lengths, inner.reshape(1)]).astype(jnp.int32)
    tok = tokens.reshape(rows, D)
    cot = cotangent.reshape(rows, D)
    cosine, sine = rotation(slots[0] * 256 + jnp.arange(256, dtype=jnp.int32))
    cosine, sine = cosine[:, 0], sine[:, 0]
    zero = jnp.zeros_like(sine)
    cos_t = jnp.concatenate([cosine, cosine, zero + 1.0, zero + 1.0], 1)
    front_t = jnp.concatenate([-sine, zero, zero, zero], 1)
    back_t = jnp.concatenate([zero, sine, zero, zero], 1)
    tables = [cos_t, front_t, back_t]
    gains = [v.reshape(1, D) for v in (gain_attn, shift_attn, gain_mlp, shift_mlp)]

    def info_in(*tokens_before):
        return (smem(), after(info, *tokens_before) if tokens_before else info)

    row_block = lambda n: block((256, n), lambda i: (i, 0))
    row_struct = lambda n, kind=BF: struct((rows, n), kind)
    tall = lambda n, index: block((256, n), index)

    head_own = jnp.concatenate(
        [w for h in range(2) for w in (w_qkv[:, h], w_out[h * 256 : (h + 1) * 256].T)], 1
    )
    head_x, head_y = along_x(head_own), along_y(head_own)
    head_c = to_core(head_own)
    in_a, in_m, grad_low, grad_sum = call(
        norm_body,
        (4,),
        [info_in(), (row_block(D), tok), (row_block(D), cot)] + [(whole(v), v) for v in gains],
        [(row_block(D), row_struct(D))] * 3 + [(block((1, D), lambda i: (0, 0)), struct((1, D), F32))],
        moved=5 * rows * D * 2,
    )
    down_own = w_down.T
    bias = jnp.swapaxes(b_qkv.reshape(2, 3, 256), 0, 1)
    head_x, head_y, head_c, in_a, in_m, grad_low, down_own, bias, *tables = bar(
        head_x, head_y, head_c, in_a, in_m, grad_low, down_own, bias, *tables
    )
    tables = [(whole(t), t) for t in tables]

    far_y, far_x = along_y(head_x[:128]), along_x(head_y[128:])
    others = [head_c, to_core(head_x), to_core(head_y)]
    far_y, far_x, up_own, *others = bar(far_y, far_x, w_up, *others)

    up_x, up_y = along_x(up_own), along_y(up_own)
    far = jnp.concatenate([far_y, far_x], 0)
    heads = both_cores(head_own, head_x, head_y, far, *others, to_core(far))
    q, kv_a, kv_b = call(
        lambda info, x, bias, *refs: qkv_body(info, x, bias.at[0], *refs),
        (3,),
        [info_in(), (whole(in_a), in_a), (block((1, 2, 256), lambda j: (j, 0, 0)), bias)]
        + tables
        + block_ins(heads, 256, lambda j: j)
        + block_ins(heads, 256, lambda j: j + 4),
        [
            (block((rows, 512), lambda j: (0, 0)), row_struct(512)),
            (block((512, 512), lambda j: (0, jnp.maximum(j - 1, 0))), struct((512, 1024), BF)),
            (block((512, 512), lambda j: (0, jnp.maximum(j - 1, 0))), struct((512, 1024), BF)),
        ],
        flops=2 * rows * D * 1536,
        moved=2 * (rows * D + D * 1536 + rows * 1536),
    )
    kv_x = along_x(kv_a)
    grad_att = call(
        grad_att_body,
        (1,),
        [info_in(q), (whole(grad_low), grad_low)]
        + block_ins(heads, 256, lambda j: 3)
        + block_ins(heads, 256, lambda j: 7),
        [(block((rows, 512), lambda j: (0, 0)), row_struct(512))],
        flops=2 * rows * D * 512,
        moved=2 * (rows * D + D * 512 + rows * 512),
    )[0]
    up_c = to_core(after(up_own, q))
    up_x, up_y, up_c, grad_att = bar(up_x, up_y, up_c, grad_att)

    up_far = along_y(up_x)
    others = [up_c, to_core(up_x), to_core(up_y)]
    down_own = after(down_own, *others)
    down_x, down_y = along_x(down_own), along_y(down_own)
    up_far, kv_x, kv_a, *others = bar(up_far, kv_x, kv_a, *others)
    ups = both_cores(up_own, up_x, up_y, up_far, *others, to_core(up_far))

    def kv_refs(own, by_x):
        both = to_core(jnp.concatenate([own, by_x], 0))
        return [(own, 0), (both, 0), (by_x, 0), (both, 2)]

    kv = [kv_refs(kv_a, kv_x)]
    act, slope = call(
        up_body,
        (4,),
        [info_in(grad_att), (whole(in_m), in_m), (block((1, 512), lambda j: (0, j)), b_up.reshape(1, -1))]
        + block_ins(ups, 512, lambda j: j),
        [(block((rows, 512), lambda j: (0, j)), row_struct(2048))] * 2,
        flops=2 * rows * D * 2048,
        moved=2 * (rows * D + D * 2048 + 2 * rows * 2048),
    )
    down_c = to_core(after(down_own, ups[7]))
    down_x, down_y, down_c, act, slope = bar(down_x, down_y, down_c, act, slope)

    def attention(part, *before):
        base = part * 2
        spot = lambda offset: block((256, 256), lambda s, h: (s + base, h + offset))
        local = lambda offset, row=0: block((256, 256), lambda s, h: (s + row, h + offset))
        return call(
            lambda *refs: attention_body(base, *refs),
            (2, 2),
            [info_in(*before), (spot(0), q), (spot(0), grad_att)]
            + tables
            + [(local(0, row), b) for b, row in kv[part]]
            + [(local(2, row), b) for b, row in kv[part]],
            [
                (local(0), struct((512, 512), BF)),
                (local(0), struct((512, 512), BF)),
                (block((1, 1, 1, 256), lambda s, h: (s, h, 0, 0)), struct((2, 2, 1, 256), F32)),
            ]
            + [(block((2, 256, 1024), lambda s, h: (0, s, 0)), struct((2, 512, 1024), BF))] * 2,
            flops=4 * 6 * 2 * 256 * 1024 * 256,
            moved=4 * 2 * 256 * 256 * 24,
        )

    def branch(part, att, *before):
        return call(
            branch_body,
            (2,),
            [
                info_in(*before),
                (block((512, 256), lambda i: (0, i)), att),
                (block((512, 1024), lambda i: (part, i)), act),
            ]
            + streamed(heads, 256, lambda i: 3 + 4 * i)
            + streamed(downs, 1024, lambda i: i),
            [(block((256, D), lambda i: (0, 0)), struct((256, D), BF))] * 2,
            scratch=[pltpu.VMEM((512, D), F32)],
            flops=2 * 512 * D * 2560,
            moved=2 * (512 * 2560 + D * 2560 + 512 * D),
        )

    top, bottom = call(
        split_body,
        (1,),
        [
            (block((128, 2048), lambda i: (0, 0)), down_x),
            (block((128, 2048), lambda i: (1, 0)), down_y),
        ],
        [(block((128, 2048), lambda i: (0, 0)), struct((128, 2048), BF))] * 2,
    )
    far_y, far_x = along_y(top), along_x(bottom)
    others = [down_c, to_core(down_x), to_core(down_y)]
    att_a, dq_a, dq_sum_a, keep_a, send_a = attention(0, top)
    far_y, far_x, att_a, kv_b, send_a, *others = bar(far_y, far_x, att_a, kv_b, send_a, *others)

    far = jnp.concatenate([far_y, far_x], 0)
    downs = both_cores(down_own, down_x, down_y, far, *others, to_core(far))
    kv_x = along_x(kv_b)
    received_a = to_core(send_a)
    branch_a = branch(0, att_a)
    received_a, *branch_a = bar(received_a, *branch_a)

    hops = Hops(info, tok, grad_low, (b_out + b_down).reshape(1, D))

    def hidden_call(before):
        return call(
            hidden_body,
            (4,),
            [info_in(before), (whole(grad_low), grad_low), (block((rows, 512), lambda j: (0, j)), slope)]
            + block_ins(downs, 512, lambda j: j),
            [
                (block((rows, 512), lambda j: (0, j)), row_struct(2048)),
                (block((1, 512), lambda j: (0, j)), struct((1, 2048), F32)),
            ],
            flops=2 * rows * D * 2048,
            moved=2 * (rows * D + D * 2048 + 2 * rows * 2048),
        )

    def project(dq, keep, came, far, before):
        return call(
            project_body,
            (1,),
            [info_in(before), (whole(dq), dq)]
            + [(pl.BlockSpec((None, 512, 1024), lambda i: (0, 0, 0)), t) for t in (keep, came)]
            + [(whole(far), far)]
            + tables,
            [
                (block((512, 1536), lambda i: (0, 0)), struct((512, 1536), BF)),
                (block((1, 1024), lambda i: (0, 0)), struct((1, 1024), F32)),
            ],
            moved=2 * 512 * 5000,
        )

    def input_part(half, low, before):
        return call(
            input_body,
            (2,),
            [
                info_in(before),
                (block((512, 768), lambda i: (0, i)), low),
                (block((512, 1024), lambda i: (half, i)), hidden_low),
                (pl.BlockSpec((512, D), lambda i: (half, 0), pipeline_mode=pl.Buffered(1)), tok),
            ]
            + [(whole(t), t) for t in (gains[0], gains[2])]
            + streamed(heads, 1024, lambda i: i)
            + streamed(ups, 1024, lambda i: i),
            [(block((256, D), lambda i: (0, 0)), struct((256, D), BF))] * 2
            + [(block((8, D), lambda i: (0, 0)), struct((8, D), F32))],
            scratch=[pltpu.VMEM((512, D), F32), pltpu.VMEM((512, D), F32), pltpu.VMEM((512, 128), F32)],
            flops=2 * 512 * D * 3584,
            moved=2 * (512 * 6000 + D * 3584),
        )

    flown = hops.start(branch_a[0])
    far_a = along_x(plus(keep_a[1], received_a[1]))
    hidden_low, b_up_sum = hidden_call(branch_a[0])
    down = Scatter([(grad_low, act)])
    down_sent = down.send(after(info, hidden_low))
    flown, kv_x, down_sent = bar(flown, kv_x, down_sent)

    flown, done = hops.land(0, flown, branch_a[1])
    kv.append(kv_refs(kv_b, after(kv_x, done)))
    down_received = to_core(after(down_sent, done))
    att_b, dq_b, dq_sum_b, keep_b, send_b = attention(1, done)
    branch_b = branch(1, att_b, att_b)
    flown, far_a, down_received, send_b, *branch_b = bar(flown, far_a, down_received, send_b, *branch_b)

    flown, done = hops.land(1, flown, branch_b[0])
    received_b = to_core(after(send_b, done))
    low_a, kv_sum_a = project(dq_a, keep_a, received_a, far_a, done)
    first, second, norm_sum_a = input_part(0, low_a, low_a)
    flown, received_b, first, second = bar(flown, received_b, first, second)

    flown, done = hops.land(2, flown, branch_b[1])
    far_b = along_x(plus(after(keep_b[1], done), received_b[1]))
    token = down.add(after(info, done), down_received)
    up = Scatter([(in_m, hidden_low)])
    up_sent = up.send(after(info, token))
    flown, far_b, up_sent = bar(flown, far_b, up_sent)

    flown, done = hops.land(3, flown, first)
    down_first = down.first(done)
    up_received = to_core(after(up_sent, done))
    low_b, kv_sum_b = project(dq_b, keep_b, received_b, far_b, done)
    third, fourth, norm_sum_b = input_part(1, low_b, low_b)
    q_sums = (dq_sum_a + dq_sum_b).sum(0).reshape(2, 1, 256)
    kv_total = (kv_sum_a + kv_sum_b).reshape(2, 2, 256)
    bias_qkv = jnp.concatenate([q_sums, kv_total], 1).reshape(-1)
    norm_sums = (norm_sum_a + norm_sum_b)[:4].reshape(-1)
    small = jnp.concatenate([norm_sums, bias_qkv, grad_sum[0], b_up_sum[0]]).reshape(-1, 128)
    flown, (down.from_x, down.from_y), up_received, third, fourth, small = bar(
        flown, down_first, up_received, third, fourth, small
    )

    flown, done = hops.land(4, flown, second)
    small_c = to_core(after(small, done))
    down_second = down.second(done)
    token = up.add(after(info, done), up_received)
    hops.write(0, token)
    project_low = jnp.concatenate([after(low_a, token), low_b], 0)
    attended = jnp.concatenate([after(att_a, token), att_b], 0)
    flown, (down.last_y, down.last_x), small_c, project_low, attended = bar(
        flown, down_second, small_c, project_low, attended
    )

    flown, done = hops.land(5, flown, third)
    up_first = up.first(done)
    attn = Scatter([(in_a, project_low), (grad_low, attended)])
    attn_sent = attn.send(after(info, done))
    small = after(small, attn_sent) + small_c
    norms = small[:64]
    norms_z = exchange(norms, "tensor", 1)
    written = hops.write(1, attn_sent)
    flown, (up.from_x, up.from_y), attn_sent, norms_z, hops.out[0] = bar(
        flown, up_first, attn_sent, norms_z, written
    )

    flown, done = hops.land(6, flown, fourth)
    attn_received = to_core(after(attn_sent, done))
    up_second = up.second(done)
    token = attn.add(after(info, done), attn_received)
    norms = after(norms, token) + norms_z
    norms_z = exchange(norms, "tensor", 2)
    flown, (up.last_y, up.last_x), norms_z, token = bar(flown, up_second, norms_z, token)

    flown, done = hops.land(7, flown)
    attn_first = attn.first(done)
    down_grad = down.total(after(info, done), True)
    written = hops.write(2, down_grad)
    written = hops.write(3, written)
    written = hops.write(4, written)
    up_grad = up.total(after(info, written))
    flown, (attn.from_x, attn.from_y), up_grad, down_grad, hops.out[1] = bar(
        flown, attn_first, up_grad, down_grad, hops.out[1]
    )

    flown, done = hops.land(8, flown)
    attn_second = attn.second(done)
    written = hops.write(5, done)
    written = hops.write(6, written)
    small = jnp.concatenate([after(norms, written) + norms_z, small[64:]], 0)
    small = small + along_y(small)
    small = small + along_x(small)
    attn.last_y, attn.last_x = attn_second
    tall = lambda array, row: (block((256, 1024), lambda i: (row, 0)), array)
    qkv_grad, out_grad = call(
        finish_body,
        (1,),
        [
            info_in(written),
            (whole(attn.own), attn.own),
            tall(attn.from_x, 0),
            tall(attn.last_y, 0),
            tall(attn.from_y, 1),
            tall(attn.last_x, 0),
        ],
        [
            (block((256, 2, 768), lambda i: (0, 0, 0)), struct((256, 2, 768), F32)),
            (block((512, 256), lambda i: (0, 0)), struct((512, 256), F32)),
        ],
    )
    hops.ready[7] = (hops.leaving, flown[0])
    (leaving, came), qkv_grad, out_grad, small, hops.out[1] = bar(
        hops.ready[7], qkv_grad, out_grad, small, hops.out[1]
    )
    hops.ready[7] = (leaving, came)
    hops.write(7, came)
    mixed, tokens_grad = hops.out

    norms = small[:64].reshape(4, D)
    small = small[64:].reshape(-1)
    bias_out = small[1536 : 1536 + D]

    return (
        mixed.reshape(tokens.shape),
        tokens_grad.reshape(tokens.shape),
        norms[0],
        norms[1],
        norms[2],
        norms[3],
        qkv_grad,
        small[:1536].reshape(b_qkv.shape),
        out_grad,
        bias_out,
        up_grad,
        small[1536 + D :],
        down_grad,
        bias_out,
    )


def solution(mesh):
    in_specs = (
        P("batch", "seq", None),
        P("batch", "seq", None),
        P("batch"),
        P(),
        P(),
        P(),
        P(),
        P(),
        P(("seq", "batch"), "tensor", None),
        P("tensor", None),
        P("tensor", ("seq", "batch")),
        P(),
        P(("seq", "batch"), "tensor"),
        P("tensor"),
        P("tensor", ("seq", "batch")),
        P(),
    )
    out_specs = (
        P("batch", "seq", None),
        P("batch", "seq", None),
        P(),
        P(),
        P(),
        P(),
        P(("seq", "batch"), "tensor", None),
        P("tensor", None),
        P("tensor", ("seq", "batch")),
        P(),
        P(("seq", "batch"), "tensor"),
        P("tensor"),
        P("tensor", ("seq", "batch")),
        P(),
    )
    links = tuple(mesh.shape[axis] for axis in ("seq", "batch", "tensor"))
    per_device = per_device_links if links == (4, 2, 4) else per_device_any
    return jax.shard_map(
        per_device, mesh=mesh, in_specs=in_specs, out_specs=out_specs, check_vma=False
    )
```

profile of v0, /device:TPU:0, one launch (start us, length us, event | category | flops | bytes accessed | tf_op | source)
XLA Modules:
  0.0 486.0 jit_solution(9816677358267317662)
XLA Ops:
  17.0 11.4 %shard_map.263 = (bf16[1024,2048]{1,0:T(8,128)(2,1)}, bf16[1024,2048]{1,0:T(8,128)(2,1)}, bf16[1024,2048]{1,0:T(8,128)(2,1)}, f32[1,2048]{1,0:T(1,128)}) custom-call(s32[10]{0:T(128)} %concatenate.49.info.refs_0_, bf16[1024,2048]{1,0:T(8,128)(2,1)} %bitcast.52, bf16[1024,2048]{1,0:T(8,128)(2,1)} %bitcast.67, f32[1,2048]{1,0:T(1,128)} %bitcast.75, ...), custom_call_target="tpu_custom_call" | custom-call | tf_op jit(solution)/shard_map/pallas_call | solution.py:251
  34.3 11.8 %collective-permute-done.3 = bf16[128,2048]{1,0:T(8,128)(2,1)S(1)} collective-permute-done((bf16[128,2048]{1,0:T(8,128)(2,1)S(1)}, bf16[128,2048]{1,0:T(8,128)(2,1)S(1)}, u32[]{:S(2)}, u32[]{:S(2)}) %collective-permute-start.3) | collective-permute-done | bytes 524320 | tf_op jit(solution)/shard_map/ppermute | solution.py:219
  50.4 13.1 %shard_map.264 = (bf16[1024,512]{1,0:T(8,128)(2,1)}, bf16[512,1024]{1,0:T(8,128)(2,1)}, bf16[512,1024]{1,0:T(8,128)(2,1)}) custom-call(s32[10]{0:T(128)} %concatenate.49.info.refs_0_, bf16[1024,2048]{1,0:T(8,128)(2,1)} %get-tuple-element.247.x.refs_0_, f32[3,2,256]{2,1,0:T(2,128)} %bitcast.86, f32[256,128]{1,0:T(8,128)} %get-tuple-element.249.refs_0_.refs_3_.cos, ...), custom_call_target="tpu_custom_call" | custom-call | tf_op jit(solution)/shard_map/pallas_call | solution.py:251
  64.3 6.3 %shard_map.265.refs_2_ = bf16[1024,512]{1,0:T(8,128)(2,1)} custom-call(s32[10]{0:T(128)} %concatenate.49.info.refs_0_, bf16[1024,2048]{1,0:T(8,128)(2,1)} %get-tuple-element.260.g.refs_0_.refs_2_.grad, bf16[256,2048]{1,0:T(8,128)(2,1)} %copy-done, bf16[256,2048]{1,0:T(8,128)(2,1)} %copy-done.2, ...), custom_call_target="tpu_custom_call" | custom-call | tf_op jit(solution)/shard_map/pallas_call | solution.py:251
  70.6 4.1 collective-permute-done.7.refs_4_.refs_10_
  75.8 20.1 %collective-permute-done.16.refs_8_.refs_12_ = bf16[512,1024]{1,0:T(8,128)(2,1)S(1)} collective-permute-done((bf16[512,1024]{1,0:T(8,128)(2,1)}, bf16[512,1024]{1,0:T(8,128)(2,1)S(1)}, u32[]{:S(2)}, u32[]{:S(2)}) %collective-permute-start.16) | collective-permute-done | bytes 1048608 | tf_op jit(solution)/shard_map/ppermute | solution.py:219
  95.9 4.7 collective-permute-done.15.refs_5_.refs_14_
  106.3 16.9 %shard_map.266 = (bf16[1024,2048]{1,0:T(8,128)(2,1)}, bf16[1024,2048]{1,0:T(8,128)(2,1)}) custom-call(s32[10]{0:T(128)} %concatenate.49.info.refs_0_, bf16[1024,2048]{1,0:T(8,128)(2,1)} %get-tuple-element.270.x.refs_0_, f32[1,2048]{1,0:T(1,128)} %bitcast.85, bf16[256,2048]{1,0:T(8,128)(2,1)} %refs_8_.1, ...), custom_call_target="tpu_custom_call" | custom-call | tf_op jit(solution)/shard_map/pallas_call | solution.py:251
  132.6 10.3 %shard_map.268 = (bf16[512,512]{1,0:T(8,128)(2,1)}, bf16[512,512]{1,0:T(8,128)(2,1)}, f32[2,2,1,256]{3,2,1,0:T(1,128)}, bf16[2,512,1024]{2,1,0:T(8,128)(2,1)}, bf16[2,512,1024]{2,1,0:T(8,128)(2,1)}) custom-call(s32[10]{0:T(128)} %concatenate.49.info.refs_0_, bf16[1024,512]{1,0:T(8,128)(2,1)} %get-tuple-element.257.refs_1_, ...), custom_call_target="tpu_custom_call" | custom-call | tf_op jit(solution)/shard_map/pallas_call | solution.py:251
  151.3 10.3 %shard_map.269 = (bf16[256,2048]{1,0:T(8,128)(2,1)}, bf16[256,2048]{1,0:T(8,128)(2,1)}) custom-call(s32[10]{0:T(128)} %concatenate.49.info.refs_0_, bf16[512,512]{1,0:T(8,128)(2,1)} %get-tuple-element.389.att, bf16[1024,2048]{1,0:T(8,128)(2,1)} %get-tuple-element.289.act.refs_1_, bf16[256,2048]{1,0:T(8,128)(2,1)} %copy-done, ...), custom_call_target="tpu_custom_call" | custom-call | tf_op jit(solution)/shard_map/pallas_call | solution.py:251
  163.3 14.4 %shard_map.270 = (bf16[1024,2048]{1,0:T(8,128)(2,1)}, f32[1,2048]{1,0:T(1,128)}) custom-call(s32[10]{0:T(128)} %concatenate.49.info.refs_0_, bf16[1024,2048]{1,0:T(8,128)(2,1)} %get-tuple-element.260.g.refs_0_.refs_2_.grad, bf16[1024,2048]{1,0:T(8,128)(2,1)} %get-tuple-element.301.slope, bf16[256,2048]{1,0:T(8,128)(2,1)} %bitcast.62, ...), custom_call_target="tpu_custom_call" | custom-call | tf_op jit(solution)/shard_map/pallas_call | solution.py:251
  177.7 9.4 %shard_map.271 = bf16[1024,2048]{1,0:T(8,128)(2,1)} custom-call(s32[10]{0:T(128)} %concatenate.49.info.refs_0_, bf16[1024,2048]{1,0:T(8,128)(2,1)} %get-tuple-element.260.g.refs_0_.refs_2_.grad, bf16[1024,2048]{1,0:T(8,128)(2,1)} %get-tuple-element.289.act.refs_1_), custom_call_target="tpu_custom_call" | custom-call | tf_op jit(solution)/shard_map/pallas_call | solution.py:265
  202.1 9.9 %shard_map.273 = (bf16[512,512]{1,0:T(8,128)(2,1)}, bf16[512,512]{1,0:T(8,128)(2,1)}, f32[2,2,1,256]{3,2,1,0:T(1,128)}, bf16[2,512,1024]{2,1,0:T(8,128)(2,1)}, bf16[2,512,1024]{2,1,0:T(8,128)(2,1)}) custom-call(s32[10]{0:T(128)} %concatenate.49.info.refs_0_, bf16[1024,512]{1,0:T(8,128)(2,1)} %get-tuple-element.257.refs_1_, ...), custom_call_target="tpu_custom_call" | custom-call | tf_op jit(solution)/shard_map/pallas_call | solution.py:251
  212.0 10.3 %shard_map.274 = (bf16[256,2048]{1,0:T(8,128)(2,1)}, bf16[256,2048]{1,0:T(8,128)(2,1)}) custom-call(s32[10]{0:T(128)} %concatenate.49.info.refs_0_, bf16[512,512]{1,0:T(8,128)(2,1)} %get-tuple-element.314.att, bf16[1024,2048]{1,0:T(8,128)(2,1)} %get-tuple-element.289.act.refs_1_, bf16[256,2048]{1,0:T(8,128)(2,1)} %copy-done, ...), custom_call_target="tpu_custom_call" | custom-call | tf_op jit(solution)/shard_map/pallas_call | solution.py:251
  226.2 3.9 collective-permute-start.33
  233.0 4.1 shard_map.276
  237.1 18.1 %shard_map.277 = (bf16[256,2048]{1,0:T(8,128)(2,1)}, bf16[256,2048]{1,0:T(8,128)(2,1)}, f32[8,2048]{1,0:T(8,128)}) custom-call(s32[10]{0:T(128)} %concatenate.49.info.refs_0_, bf16[512,1536]{1,0:T(8,128)(2,1)} %get-tuple-element.388.low, bf16[1024,2048]{1,0:T(8,128)(2,1)} %get-tuple-element.302.hid.refs_1_, bf16[1024,2048]{1,0:T(8,128)(2,1)} %bitcast.53, ...), custom_call_target="tpu_custom_call" | custom-call | tf_op jit(solution)/shard_map/pallas_call | solution.py:251
  255.2 4.4 shard_map.278
  264.8 10.9 %shard_map.279 = (bf16[512,1024]{1,0:T(8,128)(2,1)}, bf16[512,1024]{1,0:T(8,128)(2,1)}, bf16[256,1024]{1,0:T(8,128)(2,1)}, bf16[256,1024]{1,0:T(8,128)(2,1)}, bf16[256,2048]{1,0:T(8,128)(2,1)}) custom-call(s32[10]{0:T(128)} %concatenate.49.info.refs_0_, bf16[1024,2048]{1,0:T(8,128)(2,1)} %get-tuple-element.260.g.refs_0_.refs_2_.grad, ...), custom_call_target="tpu_custom_call" | custom-call | tf_op jit(solution)/shard_map/pallas_call | solution.py:265
  275.7 9.4 %shard_map.280 = bf16[1024,2048]{1,0:T(8,128)(2,1)} custom-call(s32[10]{0:T(128)} %concatenate.49.info.refs_0_, bf16[1024,2048]{1,0:T(8,128)(2,1)} %get-tuple-element.270.x.refs_0_, bf16[1024,2048]{1,0:T(8,128)(2,1)} %get-tuple-element.302.hid.refs_1_), custom_call_target="tpu_custom_call" | custom-call | tf_op jit(solution)/shard_map/pallas_call | solution.py:265
  300.1 4.1 shard_map.282
  304.2 18.3 %shard_map.283 = (bf16[256,2048]{1,0:T(8,128)(2,1)}, bf16[256,2048]{1,0:T(8,128)(2,1)}, f32[8,2048]{1,0:T(8,128)}) custom-call(s32[10]{0:T(128)} %concatenate.49.info.refs_0_, bf16[512,1536]{1,0:T(8,128)(2,1)} %get-tuple-element.358.low, bf16[1024,2048]{1,0:T(8,128)(2,1)} %get-tuple-element.302.hid.refs_1_, bf16[1024,2048]{1,0:T(8,128)(2,1)} %bitcast.54, ...), custom_call_target="tpu_custom_call" | custom-call | tf_op jit(solution)/shard_map/pallas_call | solution.py:251
  324.7 3.6 shard_map.284
  336.9 11.3 %shard_map.285 = (bf16[512,1024]{1,0:T(8,128)(2,1)}, bf16[512,1024]{1,0:T(8,128)(2,1)}, bf16[256,1024]{1,0:T(8,128)(2,1)}, bf16[256,1024]{1,0:T(8,128)(2,1)}, bf16[256,2048]{1,0:T(8,128)(2,1)}) custom-call(s32[10]{0:T(128)} %concatenate.49.info.refs_0_, bf16[1024,2048]{1,0:T(8,128)(2,1)} %get-tuple-element.270.x.refs_0_, ...), custom_call_target="tpu_custom_call" | custom-call | tf_op jit(solution)/shard_map/pallas_call | solution.py:265
  351.2 4.3 collective-permute-done.44.refs_2_.came
  363.6 9.7 %shard_map.287 = bf16[1024,2048]{1,0:T(8,128)(2,1)} custom-call(s32[10]{0:T(128)} %concatenate.49.info.refs_0_, bf16[1024,2048]{1,0:T(8,128)(2,1)} %get-tuple-element.247.x.refs_0_, bf16[1024,1536]{1,0:T(8,128)(2,1)} %pad_maximum_fusion.refs_1_, bf16[1024,2048]{1,0:T(8,128)(2,1)} %get-tuple-element.260.g.refs_0_.refs_2_.grad, ...), custom_call_target="tpu_custom_call" | custom-call | tf_op jit(solution)/shard_map/pallas_call | solution.py:265
  389.6 5.1 %collective-permute-start.54 = (bf16[256,2048]{1,0:T(8,128)(2,1)}, bf16[256,2048]{1,0:T(8,128)(2,1)S(1)}, u32[]{:S(2)}, u32[]{:S(2)}) collective-permute-start(bf16[256,2048]{1,0:T(8,128)(2,1)} %get-tuple-element.407.total), channel_id=1, source_target_pairs={{0,1},{1,0},{2,3},{3,2},{4,5},{5,4},{6,7},{7,6},{8,9},{9,8},{10,11... | collective-permute-start | bytes 3145736 | tf_op jit(solution)/shard_map/ppermute | solution.py:219
  401.7 11.4 %shard_map.291 = (bf16[512,1024]{1,0:T(8,128)(2,1)}, bf16[512,1024]{1,0:T(8,128)(2,1)}, bf16[256,1024]{1,0:T(8,128)(2,1)}, bf16[256,1024]{1,0:T(8,128)(2,1)}, bf16[256,2048]{1,0:T(8,128)(2,1)}) custom-call(s32[10]{0:T(128)} %concatenate.49.info.refs_0_, bf16[1024,2048]{1,0:T(8,128)(2,1)} %get-tuple-element.247.x.refs_0_, ...), custom_call_target="tpu_custom_call" | custom-call | tf_op jit(solution)/shard_map/pallas_call | solution.py:265
  414.0 5.2 %collective-permute-done.54.refs_2_.came = bf16[256,2048]{1,0:T(8,128)(2,1)S(1)} collective-permute-done((bf16[256,2048]{1,0:T(8,128)(2,1)}, bf16[256,2048]{1,0:T(8,128)(2,1)S(1)}, u32[]{:S(2)}, u32[]{:S(2)}) %collective-permute-start.54) | collective-permute-done | bytes 1048608 | tf_op jit(solution)/shard_map/ppermute | solution.py:219
  429.8 3.8 shard_map.293
  467.8 4.1 collective-permute-done.67
  477.0 3.9 shard_map.301
  (329 shorter events, 194.8 us)
Async XLA Ops:
  4.0 26.2 %collective-permute-start = (bf16[256,2048]{1,0:T(8,128)(2,1)S(1)}, bf16[256,2048]{1,0:T(8,128)(2,1)S(1)}, u32[]{:S(2)}, u32[]{:S(2)}) collective-permute-start(bf16[256,2048]{1,0:T(8,128)(2,1)S(1)} %pad_maximum_fusion.3.refs_3_.refs_11_.refs_0_.refs_8_), channel_id=1, source_target_pairs={{0,16},{8,24},{16,0},{24,8},{1,17},{9,25},{17,1},{25,9},{2,18},{10... | collective-permute-start | bytes 3145736 | tf_op jit(solution)/shard_map/ppermute | solution.py:219
  7.0 24.6 %collective-permute-start.1 = (bf16[256,2048]{1,0:T(8,128)(2,1)S(1)}, bf16[256,2048]{1,0:T(8,128)(2,1)S(1)}, u32[]{:S(2)}, u32[]{:S(2)}) collective-permute-start(bf16[256,2048]{1,0:T(8,128)(2,1)S(1)} %pad_maximum_fusion.3.refs_3_.refs_11_.refs_0_.refs_8_), channel_id=1, source_target_pairs={{0,4},{4,0},{1,5},{5,1},{2,6},{6,2},{3,7},{7,3},{8,12},{12,8},{9,1... | collective-permute-start | bytes 3145736 | tf_op jit(solution)/shard_map/ppermute | solution.py:219
  48.4 26.4 %collective-permute-start.7 = (bf16[256,2048]{1,0:T(8,128)(2,1)}, bf16[256,2048]{1,0:T(8,128)(2,1)}, u32[]{:S(2)}, u32[]{:S(2)}) collective-permute-start(bf16[256,2048]{1,0:T(8,128)(2,1)} %refs_8_.1), channel_id=1, source_target_pairs={{0,16},{8,24},{16,0},{24,8},{1,17},{9,25},{17,1},{25,9},{2,18},{10... | collective-permute-start | bytes 3145736 | tf_op jit(solution)/shard_map/ppermute | solution.py:219
  48.9 25.8 %collective-permute-start.8 = (bf16[256,2048]{1,0:T(8,128)(2,1)}, bf16[256,2048]{1,0:T(8,128)(2,1)}, u32[]{:S(2)}, u32[]{:S(2)}) collective-permute-start(bf16[256,2048]{1,0:T(8,128)(2,1)} %refs_8_.1), channel_id=1, source_target_pairs={{0,4},{4,0},{1,5},{5,1},{2,6},{6,2},{3,7},{7,3},{8,12},{12,8},{9,1... | collective-permute-start | bytes 3145736 | tf_op jit(solution)/shard_map/ppermute | solution.py:219
  63.8 32.1 %collective-permute-start.16 = (bf16[512,1024]{1,0:T(8,128)(2,1)}, bf16[512,1024]{1,0:T(8,128)(2,1)S(1)}, u32[]{:S(2)}, u32[]{:S(2)}) collective-permute-start(bf16[512,1024]{1,0:T(8,128)(2,1)} %get-tuple-element.281.refs_6_.refs_10_), channel_id=1, source_target_pairs={{0,16},{8,24},{16,0},{24,8},{1,17},{9,25},{17,1},{25,9},{2,18},{10... | collective-permute-start | bytes 3145736 | tf_op jit(solution)/shard_map/ppermute | solution.py:219
  75.3 25.3 %collective-permute-start.15 = (bf16[256,2048]{1,0:T(8,128)(2,1)}, bf16[256,2048]{1,0:T(8,128)(2,1)S(1)}, u32[]{:S(2)}, u32[]{:S(2)}) collective-permute-start(bf16[256,2048]{1,0:T(8,128)(2,1)} %collective-permute-done.7.refs_4_.refs_10_), channel_id=1, source_target_pairs={{0,4},{4,0},{1,5},{5,1},{2,6},{6,2},{3,7},{7,3},{8,12},{12,8},{9,1... | collective-permute-start | bytes 3145736 | tf_op jit(solution)/shard_map/ppermute | solution.py:219
  100.7 25.7 %collective-permute-start.13 = (bf16[256,2048]{1,0:T(8,128)(2,1)S(1)}, bf16[256,2048]{1,0:T(8,128)(2,1)}, u32[]{:S(2)}, u32[]{:S(2)}) collective-permute-start(bf16[256,2048]{1,0:T(8,128)(2,1)S(1)} %bitcast.64), channel_id=1, source_target_pairs={{0,16},{8,24},{16,0},{24,8},{1,17},{9,25},{17,1},{25,9},{2,18},{10... | collective-permute-start | bytes 3145736 | tf_op jit(solution)/shard_map/ppermute | solution.py:219
  101.3 25.3 %collective-permute-start.14 = (bf16[256,2048]{1,0:T(8,128)(2,1)S(1)}, bf16[256,2048]{1,0:T(8,128)(2,1)}, u32[]{:S(2)}, u32[]{:S(2)}) collective-permute-start(bf16[256,2048]{1,0:T(8,128)(2,1)S(1)} %bitcast.65), channel_id=1, source_target_pairs={{0,4},{4,0},{1,5},{5,1},{2,6},{6,2},{3,7},{7,3},{8,12},{12,8},{9,1... | collective-permute-start | bytes 3145736 | tf_op jit(solution)/shard_map/ppermute | solution.py:219
  105.9 25.4 %collective-permute-start.21 = (bf16[1024,1024]{1,0:T(8,128)(2,1)}, bf16[1024,1024]{1,0:T(8,128)(2,1)S(1)}, u32[]{:S(2)}, u32[]{:S(2)}) collective-permute-start(bf16[1024,1024]{1,0:T(8,128)(2,1)} %pad_maximum_fusion.1), channel_id=1, source_target_pairs={{0,8},{8,0},{16,24},{24,16},{1,9},{9,1},{17,25},{25,17},{2,10},{10... | collective-permute-start | bytes 6291464 | tf_op jit(solution)/shard_map/ppermute | solution.py:219
  146.3 40.8 %collective-permute-start.27 = (bf16[512,1024]{1,0:T(8,128)(2,1)S(1)}, bf16[512,1024]{1,0:T(8,128)(2,1)}, u32[]{:S(2)}, u32[]{:S(2)}) collective-permute-start(bf16[512,1024]{1,0:T(8,128)(2,1)S(1)} %copy-done.12), channel_id=1, source_target_pairs={{0,16},{8,24},{16,0},{24,8},{1,17},{9,25},{17,1},{25,9},{2,18},{10... | collective-permute-start | bytes 3145736 | tf_op jit(solution)/shard_map/ppermute | solution.py:219
  161.5 25.6 %collective-permute-start.26 = (bf16[256,2048]{1,0:T(8,128)(2,1)}, bf16[256,2048]{1,0:T(8,128)(2,1)S(1)}, u32[]{:S(2)}, u32[]{:S(2)}) collective-permute-start(bf16[256,2048]{1,0:T(8,128)(2,1)} %get-tuple-element.298.refs_1_), channel_id=1, source_target_pairs={{0,1},{1,0},{2,3},{3,2},{4,5},{5,4},{6,7},{7,6},{8,9},{9,8},{10,11... | collective-permute-start | bytes 3145736 | tf_op jit(solution)/shard_map/ppermute | solution.py:219
  190.6 31.8 %collective-permute-start.31 = (bf16[1024,2048]{1,0:T(8,128)(2,1)}, bf16[1024,2048]{1,0:T(8,128)(2,1)}, u32[]{:S(2)}, u32[]{:S(2)}) collective-permute-start(bf16[1024,2048]{1,0:T(8,128)(2,1)} %shard_map.271), channel_id=1, source_target_pairs={{0,8},{8,0},{16,24},{24,16},{1,9},{9,1},{17,25},{25,17},{2,10},{10... | collective-permute-start | bytes 12582920 | tf_op jit(solution)/shard_map/ppermute | solution.py:219
  195.2 27.2 %collective-permute-start.30 = (bf16[512,1024]{1,0:T(8,128)(2,1)}, bf16[512,1024]{1,0:T(8,128)(2,1)}, u32[]{:S(2)}, u32[]{:S(2)}) collective-permute-start(bf16[512,1024]{1,0:T(8,128)(2,1)} %fusion.1), channel_id=1, source_target_pairs={{0,16},{8,24},{16,0},{24,8},{1,17},{9,25},{17,1},{25,9},{2,18},{10... | collective-permute-start | bytes 3145736 | tf_op jit(solution)/shard_map/ppermute | solution.py:219
  196.6 25.7 %collective-permute-start.28 = (bf16[256,2048]{1,0:T(8,128)(2,1)}, bf16[256,2048]{1,0:T(8,128)(2,1)}, u32[]{:S(2)}, u32[]{:S(2)}) collective-permute-start(bf16[256,2048]{1,0:T(8,128)(2,1)} %get-tuple-element.305.refs_1_), channel_id=1, source_target_pairs={{0,1},{1,0},{2,3},{3,2},{4,5},{5,4},{6,7},{7,6},{8,9},{9,8},{10,11... | collective-permute-start | bytes 3145736 | tf_op jit(solution)/shard_map/ppermute | solution.py:219
  226.0 29.2 %collective-permute-start.35 = (bf16[2,512,1024]{2,1,0:T(8,128)(2,1)}, bf16[2,512,1024]{2,1,0:T(8,128)(2,1)S(1)}, u32[]{:S(2)}, u32[]{:S(2)}) collective-permute-start(bf16[2,512,1024]{2,1,0:T(8,128)(2,1)} %get-tuple-element.325), channel_id=1, source_target_pairs={{0,8},{8,0},{16,24},{24,16},{1,9},{9,1},{17,25},{25,17},{2,10},{10... | collective-permute-start | bytes 6291464 | tf_op jit(solution)/shard_map/ppermute | solution.py:219
  226.2 29.0 %collective-permute-start.33 = (bf16[256,2048]{1,0:T(8,128)(2,1)}, bf16[256,2048]{1,0:T(8,128)(2,1)}, u32[]{:S(2)}, u32[]{:S(2)}) collective-permute-start(bf16[256,2048]{1,0:T(8,128)(2,1)} %get-tuple-element.322.total), channel_id=1, source_target_pairs={{0,1},{1,0},{2,3},{3,2},{4,5},{5,4},{6,7},{7,6},{8,9},{9,8},{10,11... | collective-permute-start | bytes 3145736 | tf_op jit(solution)/shard_map/ppermute | solution.py:219
  230.0 25.2 %collective-permute-start.34 = (bf16[256,2048]{1,0:T(8,128)(2,1)}, bf16[256,2048]{1,0:T(8,128)(2,1)}, u32[]{:S(2)}, u32[]{:S(2)}) collective-permute-start(bf16[256,2048]{1,0:T(8,128)(2,1)} %get-tuple-element.323.refs_3_), channel_id=1, source_target_pairs={{1,2},{2,1},{5,6},{6,5},{9,10},{10,9},{13,14},{14,13},{17,18},{18,... | collective-permute-start | bytes 3145736 | tf_op jit(solution)/shard_map/ppermute | solution.py:691
  261.0 25.4 %collective-permute-start.38 = (bf16[512,1024]{1,0:T(8,128)(2,1)}, bf16[512,1024]{1,0:T(8,128)(2,1)S(1)}, u32[]{:S(2)}, u32[]{:S(2)}) collective-permute-start(bf16[512,1024]{1,0:T(8,128)(2,1)} %fusion), channel_id=1, source_target_pairs={{0,16},{8,24},{16,0},{24,8},{1,17},{9,25},{17,1},{25,9},{2,18},{10... | collective-permute-start | bytes 3145736 | tf_op jit(solution)/shard_map/ppermute | solution.py:219
  261.6 25.4 %collective-permute-start.36 = (bf16[256,2048]{1,0:T(8,128)(2,1)}, bf16[256,2048]{1,0:T(8,128)(2,1)S(1)}, u32[]{:S(2)}, u32[]{:S(2)}) collective-permute-start(bf16[256,2048]{1,0:T(8,128)(2,1)} %get-tuple-element.335.total), channel_id=1, source_target_pairs={{0,1},{1,0},{2,3},{3,2},{4,5},{5,4},{6,7},{7,6},{8,9},{9,8},{10,11... | collective-permute-start | bytes 3145736 | tf_op jit(solution)/shard_map/ppermute | solution.py:219
  292.5 31.1 %collective-permute-start.43 = (bf16[1024,2048]{1,0:T(8,128)(2,1)}, bf16[1024,2048]{1,0:T(8,128)(2,1)}, u32[]{:S(2)}, u32[]{:S(2)}) collective-permute-start(bf16[1024,2048]{1,0:T(8,128)(2,1)} %shard_map.280), channel_id=1, source_target_pairs={{0,8},{8,0},{16,24},{24,16},{1,9},{9,1},{17,25},{25,17},{2,10},{10... | collective-permute-start | bytes 12582920 | tf_op jit(solution)/shard_map/ppermute | solution.py:219
  292.6 31.0 %collective-permute-start.42 = (bf16[512,1024]{1,0:T(8,128)(2,1)}, bf16[512,1024]{1,0:T(8,128)(2,1)S(1)}, u32[]{:S(2)}, u32[]{:S(2)}) collective-permute-start(bf16[512,1024]{1,0:T(8,128)(2,1)} %get-tuple-element.352), channel_id=1, source_target_pairs={{0,4},{4,0},{1,5},{5,1},{2,6},{6,2},{3,7},{7,3},{8,12},{12,8},{9,1... | collective-permute-start | bytes 3145736 | tf_op jit(solution)/shard_map/ppermute | solution.py:219
  294.2 29.4 %collective-permute-start.41 = (bf16[512,1024]{1,0:T(8,128)(2,1)}, bf16[512,1024]{1,0:T(8,128)(2,1)S(1)}, u32[]{:S(2)}, u32[]{:S(2)}) collective-permute-start(bf16[512,1024]{1,0:T(8,128)(2,1)} %get-tuple-element.350), channel_id=1, source_target_pairs={{0,16},{8,24},{16,0},{24,8},{1,17},{9,25},{17,1},{25,9},{2,18},{10... | collective-permute-start | bytes 3145736 | tf_op jit(solution)/shard_map/ppermute | solution.py:219
  295.7 27.9 %collective-permute-start.39 = (bf16[256,2048]{1,0:T(8,128)(2,1)}, bf16[256,2048]{1,0:T(8,128)(2,1)S(1)}, u32[]{:S(2)}, u32[]{:S(2)}) collective-permute-start(bf16[256,2048]{1,0:T(8,128)(2,1)} %get-tuple-element.347.total), channel_id=1, source_target_pairs={{0,1},{1,0},{2,3},{3,2},{4,5},{5,4},{6,7},{7,6},{8,9},{9,8},{10,11... | collective-permute-start | bytes 3145736 | tf_op jit(solution)/shard_map/ppermute | solution.py:219
  298.4 25.3 %collective-permute-start.40 = (bf16[256,2048]{1,0:T(8,128)(2,1)}, bf16[256,2048]{1,0:T(8,128)(2,1)}, u32[]{:S(2)}, u32[]{:S(2)}) collective-permute-start(bf16[256,2048]{1,0:T(8,128)(2,1)} %get-tuple-element.348.refs_3_), channel_id=1, source_target_pairs={{1,2},{2,1},{5,6},{6,5},{9,10},{10,9},{13,14},{14,13},{17,18},{18,... | collective-permute-start | bytes 3145736 | tf_op jit(solution)/shard_map/ppermute | solution.py:691
  328.3 27.2 %collective-permute-start.45 = (bf16[256,2048]{1,0:T(8,128)(2,1)}, bf16[256,2048]{1,0:T(8,128)(2,1)}, u32[]{:S(2)}, u32[]{:S(2)}) collective-permute-start(bf16[256,2048]{1,0:T(8,128)(2,1)} %get-tuple-element.376.refs_3_), channel_id=1, source_target_pairs={{1,2},{2,1},{5,6},{6,5},{9,10},{10,9},{13,14},{14,13},{17,18},{18,... | collective-permute-start | bytes 3145736 | tf_op jit(solution)/shard_map/ppermute | solution.py:691
  330.0 25.6 %collective-permute-start.44 = (bf16[256,2048]{1,0:T(8,128)(2,1)}, bf16[256,2048]{1,0:T(8,128)(2,1)}, u32[]{:S(2)}, u32[]{:S(2)}) collective-permute-start(bf16[256,2048]{1,0:T(8,128)(2,1)} %get-tuple-element.375.total), channel_id=1, source_target_pairs={{0,1},{1,0},{2,3},{3,2},{4,5},{5,4},{6,7},{7,6},{8,9},{9,8},{10,11... | collective-permute-start | bytes 3145736 | tf_op jit(solution)/shard_map/ppermute | solution.py:219
  359.1 25.1 %collective-permute-start.52 = (bf16[512,1024]{1,0:T(8,128)(2,1)}, bf16[512,1024]{1,0:T(8,128)(2,1)S(1)}, u32[]{:S(2)}, u32[]{:S(2)}) collective-permute-start(bf16[512,1024]{1,0:T(8,128)(2,1)} %get-tuple-element.397), channel_id=1, source_target_pairs={{0,4},{4,0},{1,5},{5,1},{2,6},{6,2},{3,7},{7,3},{8,12},{12,8},{9,1... | collective-permute-start | bytes 3145736 | tf_op jit(solution)/shard_map/ppermute | solution.py:219
  359.7 24.5 %collective-permute-start.51 = (bf16[512,1024]{1,0:T(8,128)(2,1)}, bf16[512,1024]{1,0:T(8,128)(2,1)S(1)}, u32[]{:S(2)}, u32[]{:S(2)}) collective-permute-start(bf16[512,1024]{1,0:T(8,128)(2,1)} %get-tuple-element.395), channel_id=1, source_target_pairs={{0,16},{8,24},{16,0},{24,8},{1,17},{9,25},{17,1},{25,9},{2,18},{10... | collective-permute-start | bytes 3145736 | tf_op jit(solution)/shard_map/ppermute | solution.py:219
  388.9 30.3 %collective-permute-start.55 = (bf16[256,2048]{1,0:T(8,128)(2,1)}, bf16[256,2048]{1,0:T(8,128)(2,1)S(1)}, u32[]{:S(2)}, u32[]{:S(2)}) collective-permute-start(bf16[256,2048]{1,0:T(8,128)(2,1)} %get-tuple-element.408.refs_3_), channel_id=1, source_target_pairs={{1,2},{2,1},{5,6},{6,5},{9,10},{10,9},{13,14},{14,13},{17,18},{18,... | collective-permute-start | bytes 3145736 | tf_op jit(solution)/shard_map/ppermute | solution.py:691
  389.6 29.5 %collective-permute-start.54 = (bf16[256,2048]{1,0:T(8,128)(2,1)}, bf16[256,2048]{1,0:T(8,128)(2,1)S(1)}, u32[]{:S(2)}, u32[]{:S(2)}) collective-permute-start(bf16[256,2048]{1,0:T(8,128)(2,1)} %get-tuple-element.407.total), channel_id=1, source_target_pairs={{0,1},{1,0},{2,3},{3,2},{4,5},{5,4},{6,7},{7,6},{8,9},{9,8},{10,11... | collective-permute-start | bytes 3145736 | tf_op jit(solution)/shard_map/ppermute | solution.py:219
  423.8 24.6 %collective-permute-start.63 = (bf16[512,1024]{1,0:T(8,128)(2,1)}, bf16[512,1024]{1,0:T(8,128)(2,1)S(1)}, u32[]{:S(2)}, u32[]{:S(2)}) collective-permute-start(bf16[512,1024]{1,0:T(8,128)(2,1)} %get-tuple-element.434), channel_id=1, source_target_pairs={{0,4},{4,0},{1,5},{5,1},{2,6},{6,2},{3,7},{7,3},{8,12},{12,8},{9,1... | collective-permute-start | bytes 3145736 | tf_op jit(solution)/shard_map/ppermute | solution.py:219
  454.3 26.7 %collective-permute-start.64 = (bf16[256,2048]{1,0:T(8,128)(2,1)}, bf16[256,2048]{1,0:T(8,128)(2,1)S(1)}, u32[]{:S(2)}, u32[]{:S(2)}) collective-permute-start(bf16[256,2048]{1,0:T(8,128)(2,1)} %shard_map.298.total), channel_id=1, source_target_pairs={{0,1},{1,0},{2,3},{3,2},{4,5},{5,4},{6,7},{7,6},{8,9},{9,8},{10,11... | collective-permute-start | bytes 3145736 | tf_op jit(solution)/shard_map/ppermute | solution.py:219
  (98 other events, 1119.8 us)
where the time goes:
time: 490 us; the launch traced here: 486 us
  Pallas kernels  277 us (57%)
  waiting for transfers between devices  80.8 us (16%)
  starting transfers between devices  74 us (15%)
  local copies, waits for them, and re-layouts  28.9 us (6%)
  other arithmetic  23.1 us (5%)
    pallas_call x34, Pallas kernels, call(): pl.pallas_call(body, grid=grid, in_specs=[spec for spec, _ in ins], out_s...  215 us
    ppermute x61, waiting for transfers between devices, exchange(): return lax.ppermute(array, axis, [(i, i ^ flip) for i in range(size)])  80.8 us
    ppermute x61, starting transfers between devices, exchange(): return lax.ppermute(array, axis, [(i, i ^ flip) for i in range(size)])  62.6 us
    pallas_call x6, Pallas kernels, call_placed(): pl.pallas_call(body, grid_spec=pltpu.PrefetchScalarGridSpec(num_scalar_pr...  62.1 us
    unnamed x129, local copies, waits for them, and re-layouts  18 us
    convert_element_type x8, other arithmetic, plus(): return (a.astype(F32) + b.astype(F32)).astype(BF)  13.4 us
    ppermute x8, starting transfers between devices, land(): flying.append(lax.ppermute(pair, 'tensor', [(1, 2), (2, 1)]))  11.3 us
  transfers between devices with their start and end apart: 69, of which 26 were waited for; matrix products, arithmetic and copies ran while one was open for 6% of the time, Pallas kernels for 50%

commit v1 on v0

--- a/solution.py
+++ b/solution.py
@@ -239,7 +239,11 @@
 
 
 def block_ins(blocks, width, column):
-    return [(pl.BlockSpec((256, width), lambda j: (0, column(j))), b) for b in blocks]
+    return [(pl.BlockSpec((b.shape[0], width), lambda j: (0, column(j))), b) for b in flat(blocks)]
+
+
+def flat(blocks):
+    return [half for b in blocks for half in (b if isinstance(b, tuple) else (b,))]
 
 
 def both_cores(own, by_x, by_y, far, *others):
@@ -383,8 +387,8 @@
 
 
 def hidden_body(info, g, slope, *refs):
-    low, total = refs[8:]
-    grad = matched(g, refs[:8], info) * slope[...].astype(F32)
+    low, total = refs[-2:]
+    grad = matched(g, refs[:-2], info) * slope[...].astype(F32)
     low[...] = grad.astype(BF)
     total[...] = jnp.sum(grad, 0, keepdims=True)
 
@@ -441,15 +445,20 @@
 
 
 def streamed(blocks, width, column):
-    return [(pl.BlockSpec((256, width), lambda i: (0, column(i))), blocks[r]) for r in ORDER]
+    ordered = flat([blocks[r] for r in ORDER])
+    return [(pl.BlockSpec((b.shape[0], width), lambda i: (0, column(i))), b) for b in ordered]
 
 
 def branch_body(info, att, act, *refs):
-    w_att, w_act, outs, total = refs[:8], refs[8:16], refs[16:18], refs[18]
+    w_att, w_act, outs, total = refs[:8], refs[8:18], refs[18:20], refs[20]
     step = pl.program_id(0)
 
     def part(i):
-        return nt(att[...], w_att[i][...]) + nt(act[...], w_act[i][...])
+        if i < 6:
+            w = w_act[i][...]
+        else:
+            w = jnp.concatenate([w_act[2 * i - 6][...], w_act[2 * i - 5][...]], 0)
+        return nt(att[...], w_att[i][...]) + nt(act[...], w)
 
     @pl.when(step == 0)
     def _():
@@ -906,8 +915,8 @@
     att_a, dq_a, dq_sum_a, keep_a, send_a = attention(0, top)
     far_y, far_x, att_a, kv_b, send_a, *others = bar(far_y, far_x, att_a, kv_b, send_a, *others)
 
-    far = jnp.concatenate([far_y, far_x], 0)
-    downs = both_cores(down_own, down_x, down_y, far, *others, to_core(far))
+    halves = (far_y, far_x)
+    downs = both_cores(down_own, down_x, down_y, halves, *others, tuple(to_core(half) for half in halves))
     kv_x = along_x(kv_b)
     received_a = to_core(send_a)
     branch_a = branch(0, att_a)

time: 490 us -> 489 us (level)
    ppermute x61 -> x62, waiting for transfers between devices: 80.8 us -> 82.6 us  [exchange(): return lax.ppermute(array, axis, [(i, i ^ flip) for i in range(size)])]
    ppermute x61 -> x62, starting transfers between devices: 62.6 us -> 62.2 us  [exchange(): return lax.ppermute(array, axis, [(i, i ^ flip) for i in range(size)])]
    unnamed x129 -> x132, local copies, waits for them, and re-layouts: 18 us -> 17.7 us
  transfers between devices with their start and end apart: 69 -> 70, of which waited for: 26 -> 29; matrix products, arithmetic and copies ran while one was open for 6% -> 6% of each run, Pallas kernels for 50% -> 50%
where the time goes in v1:
time: 489 us; the launch traced here: 485 us
  Pallas kernels  277 us (57%)
  waiting for transfers between devices  82.6 us (17%)
  starting transfers between devices  73.4 us (15%)
  local copies, waits for them, and re-layouts  27.4 us (6%)
  other arithmetic  21.8 us (4%)
    pallas_call x34, Pallas kernels, call(): pl.pallas_call(body, grid=grid, in_specs=[spec for spec, _ in ins], out_s...  215 us
    ppermute x62, waiting for transfers between devices, exchange(): return lax.ppermute(array, axis, [(i, i ^ flip) for i in range(size)])  82.6 us
    pallas_call x6, Pallas kernels, call_placed(): pl.pallas_call(body, grid_spec=pltpu.PrefetchScalarGridSpec(num_scalar_pr...  62.2 us
    ppermute x62, starting transfers between devices, exchange(): return lax.ppermute(array, axis, [(i, i ^ flip) for i in range(size)])  62.2 us
    unnamed x132, local copies, waits for them, and re-layouts  17.7 us
    convert_element_type x8, other arithmetic, plus(): return (a.astype(F32) + b.astype(F32)).astype(BF)  13.5 us
    ppermute x8, starting transfers between devices, land(): flying.append(lax.ppermute(pair, 'tensor', [(1, 2), (2, 1)]))  11.3 us
  transfers between devices with their start and end apart: 70, of which 29 were waited for; matrix products, arithmetic and copies ran while one was open for 6% of the time, Pallas kernels for 50%

profile of v1, /device:TPU:0, one launch (start us, length us, event | category | flops | bytes accessed | tf_op | source)
XLA Modules:
  0.0 484.8 jit_solution(17785278340738879269)
XLA Ops:
  17.0 11.4 %shard_map.263 = (bf16[1024,2048]{1,0:T(8,128)(2,1)}, bf16[1024,2048]{1,0:T(8,128)(2,1)}, bf16[1024,2048]{1,0:T(8,128)(2,1)}, f32[1,2048]{1,0:T(1,128)}) custom-call(s32[10]{0:T(128)} %concatenate.46.info.refs_0_, bf16[1024,2048]{1,0:T(8,128)(2,1)} %bitcast.52, bf16[1024,2048]{1,0:T(8,128)(2,1)} %bitcast.67, f32[1,2048]{1,0:T(1,128)} %bitcast.75, ...), custom_call_target="tpu_custom_call" | custom-call | tf_op jit(solution)/shard_map/pallas_call | solution.py:255
  34.3 11.8 %collective-permute-done.3 = bf16[128,2048]{1,0:T(8,128)(2,1)S(1)} collective-permute-done((bf16[128,2048]{1,0:T(8,128)(2,1)S(1)}, bf16[128,2048]{1,0:T(8,128)(2,1)S(1)}, u32[]{:S(2)}, u32[]{:S(2)}) %collective-permute-start.3) | collective-permute-done | bytes 524320 | tf_op jit(solution)/shard_map/ppermute | solution.py:219
  50.4 13.1 %shard_map.264 = (bf16[1024,512]{1,0:T(8,128)(2,1)}, bf16[512,1024]{1,0:T(8,128)(2,1)}, bf16[512,1024]{1,0:T(8,128)(2,1)}) custom-call(s32[10]{0:T(128)} %concatenate.46.info.refs_0_, bf16[1024,2048]{1,0:T(8,128)(2,1)} %get-tuple-element.247.x.refs_0_, f32[3,2,256]{2,1,0:T(2,128)} %bitcast.86, f32[256,128]{1,0:T(8,128)} %get-tuple-element.249.refs_0_.refs_3_.cos, ...), custom_call_target="tpu_custom_call" | custom-call | tf_op jit(solution)/shard_map/pallas_call | solution.py:255
  64.3 6.3 %shard_map.265.refs_2_ = bf16[1024,512]{1,0:T(8,128)(2,1)} custom-call(s32[10]{0:T(128)} %concatenate.46.info.refs_0_, bf16[1024,2048]{1,0:T(8,128)(2,1)} %get-tuple-element.260.g.refs_0_.refs_2_.grad, bf16[256,2048]{1,0:T(8,128)(2,1)} %copy-done, bf16[256,2048]{1,0:T(8,128)(2,1)} %copy-done.2, ...), custom_call_target="tpu_custom_call" | custom-call | tf_op jit(solution)/shard_map/pallas_call | solution.py:255
  70.6 4.2 collective-permute-done.7.refs_4_.refs_10_
  75.8 20.1 %collective-permute-done.16.refs_8_.refs_12_ = bf16[512,1024]{1,0:T(8,128)(2,1)S(1)} collective-permute-done((bf16[512,1024]{1,0:T(8,128)(2,1)}, bf16[512,1024]{1,0:T(8,128)(2,1)S(1)}, u32[]{:S(2)}, u32[]{:S(2)}) %collective-permute-start.16) | collective-permute-done | bytes 1048608 | tf_op jit(solution)/shard_map/ppermute | solution.py:219
  95.9 4.7 collective-permute-done.15.refs_5_.refs_14_
  106.3 16.9 %shard_map.266 = (bf16[1024,2048]{1,0:T(8,128)(2,1)}, bf16[1024,2048]{1,0:T(8,128)(2,1)}) custom-call(s32[10]{0:T(128)} %concatenate.46.info.refs_0_, bf16[1024,2048]{1,0:T(8,128)(2,1)} %get-tuple-element.270.x.refs_0_, f32[1,2048]{1,0:T(1,128)} %bitcast.85, bf16[256,2048]{1,0:T(8,128)(2,1)} %refs_8_.1, ...), custom_call_target="tpu_custom_call" | custom-call | tf_op jit(solution)/shard_map/pallas_call | solution.py:255
  132.6 10.3 %shard_map.268 = (bf16[512,512]{1,0:T(8,128)(2,1)}, bf16[512,512]{1,0:T(8,128)(2,1)}, f32[2,2,1,256]{3,2,1,0:T(1,128)}, bf16[2,512,1024]{2,1,0:T(8,128)(2,1)}, bf16[2,512,1024]{2,1,0:T(8,128)(2,1)}) custom-call(s32[10]{0:T(128)} %concatenate.46.info.refs_0_, bf16[1024,512]{1,0:T(8,128)(2,1)} %get-tuple-element.257.refs_1_, ...), custom_call_target="tpu_custom_call" | custom-call | tf_op jit(solution)/shard_map/pallas_call | solution.py:255
  150.6 10.3 %shard_map.269 = (bf16[256,2048]{1,0:T(8,128)(2,1)}, bf16[256,2048]{1,0:T(8,128)(2,1)}) custom-call(s32[10]{0:T(128)} %concatenate.46.info.refs_0_, bf16[512,512]{1,0:T(8,128)(2,1)} %get-tuple-element.389.att, bf16[1024,2048]{1,0:T(8,128)(2,1)} %get-tuple-element.289.act.refs_1_, bf16[256,2048]{1,0:T(8,128)(2,1)} %copy-done, ...), custom_call_target="tpu_custom_call" | custom-call | tf_op jit(solution)/shard_map/pallas_call | solution.py:255
  162.6 14.5 %shard_map.270 = (bf16[1024,2048]{1,0:T(8,128)(2,1)}, f32[1,2048]{1,0:T(1,128)}) custom-call(s32[10]{0:T(128)} %concatenate.46.info.refs_0_, bf16[1024,2048]{1,0:T(8,128)(2,1)} %get-tuple-element.260.g.refs_0_.refs_2_.grad, bf16[1024,2048]{1,0:T(8,128)(2,1)} %get-tuple-element.301.slope, bf16[256,2048]{1,0:T(8,128)(2,1)} %bitcast.62, ...), custom_call_target="tpu_custom_call" | custom-call | tf_op jit(solution)/shard_map/pallas_call | solution.py:255
  177.1 9.4 %shard_map.271 = bf16[1024,2048]{1,0:T(8,128)(2,1)} custom-call(s32[10]{0:T(128)} %concatenate.46.info.refs_0_, bf16[1024,2048]{1,0:T(8,128)(2,1)} %get-tuple-element.260.g.refs_0_.refs_2_.grad, bf16[1024,2048]{1,0:T(8,128)(2,1)} %get-tuple-element.289.act.refs_1_), custom_call_target="tpu_custom_call" | custom-call | tf_op jit(solution)/shard_map/pallas_call | solution.py:269
  201.3 10.0 %shard_map.273 = (bf16[512,512]{1,0:T(8,128)(2,1)}, bf16[512,512]{1,0:T(8,128)(2,1)}, f32[2,2,1,256]{3,2,1,0:T(1,128)}, bf16[2,512,1024]{2,1,0:T(8,128)(2,1)}, bf16[2,512,1024]{2,1,0:T(8,128)(2,1)}) custom-call(s32[10]{0:T(128)} %concatenate.46.info.refs_0_, bf16[1024,512]{1,0:T(8,128)(2,1)} %get-tuple-element.257.refs_1_, ...), custom_call_target="tpu_custom_call" | custom-call | tf_op jit(solution)/shard_map/pallas_call | solution.py:255
  211.3 10.3 %shard_map.274 = (bf16[256,2048]{1,0:T(8,128)(2,1)}, bf16[256,2048]{1,0:T(8,128)(2,1)}) custom-call(s32[10]{0:T(128)} %concatenate.46.info.refs_0_, bf16[512,512]{1,0:T(8,128)(2,1)} %get-tuple-element.314.att, bf16[1024,2048]{1,0:T(8,128)(2,1)} %get-tuple-element.289.act.refs_1_, bf16[256,2048]{1,0:T(8,128)(2,1)} %copy-done, ...), custom_call_target="tpu_custom_call" | custom-call | tf_op jit(solution)/shard_map/pallas_call | solution.py:255
  221.7 3.7 shard_map.275
  231.6 4.2 shard_map.276
  235.8 18.1 %shard_map.277 = (bf16[256,2048]{1,0:T(8,128)(2,1)}, bf16[256,2048]{1,0:T(8,128)(2,1)}, f32[8,2048]{1,0:T(8,128)}) custom-call(s32[10]{0:T(128)} %concatenate.46.info.refs_0_, bf16[512,1536]{1,0:T(8,128)(2,1)} %get-tuple-element.388.low, bf16[1024,2048]{1,0:T(8,128)(2,1)} %get-tuple-element.302.hid.refs_1_, bf16[1024,2048]{1,0:T(8,128)(2,1)} %bitcast.53, ...), custom_call_target="tpu_custom_call" | custom-call | tf_op jit(solution)/shard_map/pallas_call | solution.py:255
  253.9 4.3 shard_map.278
  263.9 10.9 %shard_map.279 = (bf16[512,1024]{1,0:T(8,128)(2,1)}, bf16[512,1024]{1,0:T(8,128)(2,1)}, bf16[256,1024]{1,0:T(8,128)(2,1)}, bf16[256,1024]{1,0:T(8,128)(2,1)}, bf16[256,2048]{1,0:T(8,128)(2,1)}) custom-call(s32[10]{0:T(128)} %concatenate.46.info.refs_0_, bf16[1024,2048]{1,0:T(8,128)(2,1)} %get-tuple-element.260.g.refs_0_.refs_2_.grad, ...), custom_call_target="tpu_custom_call" | custom-call | tf_op jit(solution)/shard_map/pallas_call | solution.py:269
  274.8 9.4 %shard_map.280 = bf16[1024,2048]{1,0:T(8,128)(2,1)} custom-call(s32[10]{0:T(128)} %concatenate.46.info.refs_0_, bf16[1024,2048]{1,0:T(8,128)(2,1)} %get-tuple-element.270.x.refs_0_, bf16[1024,2048]{1,0:T(8,128)(2,1)} %get-tuple-element.302.hid.refs_1_), custom_call_target="tpu_custom_call" | custom-call | tf_op jit(solution)/shard_map/pallas_call | solution.py:269
  298.7 4.1 shard_map.282
  302.9 18.4 %shard_map.283 = (bf16[256,2048]{1,0:T(8,128)(2,1)}, bf16[256,2048]{1,0:T(8,128)(2,1)}, f32[8,2048]{1,0:T(8,128)}) custom-call(s32[10]{0:T(128)} %concatenate.46.info.refs_0_, bf16[512,1536]{1,0:T(8,128)(2,1)} %get-tuple-element.358.low, bf16[1024,2048]{1,0:T(8,128)(2,1)} %get-tuple-element.302.hid.refs_1_, bf16[1024,2048]{1,0:T(8,128)(2,1)} %bitcast.54, ...), custom_call_target="tpu_custom_call" | custom-call | tf_op jit(solution)/shard_map/pallas_call | solution.py:255
  323.4 3.6 shard_map.284
  335.9 11.3 %shard_map.285 = (bf16[512,1024]{1,0:T(8,128)(2,1)}, bf16[512,1024]{1,0:T(8,128)(2,1)}, bf16[256,1024]{1,0:T(8,128)(2,1)}, bf16[256,1024]{1,0:T(8,128)(2,1)}, bf16[256,2048]{1,0:T(8,128)(2,1)}) custom-call(s32[10]{0:T(128)} %concatenate.46.info.refs_0_, bf16[1024,2048]{1,0:T(8,128)(2,1)} %get-tuple-element.270.x.refs_0_, ...), custom_call_target="tpu_custom_call" | custom-call | tf_op jit(solution)/shard_map/pallas_call | solution.py:269
  350.3 4.0 collective-permute-done.45.refs_2_.came
  362.8 9.7 %shard_map.287 = bf16[1024,2048]{1,0:T(8,128)(2,1)} custom-call(s32[10]{0:T(128)} %concatenate.46.info.refs_0_, bf16[1024,2048]{1,0:T(8,128)(2,1)} %get-tuple-element.247.x.refs_0_, bf16[1024,1536]{1,0:T(8,128)(2,1)} %pad_maximum_fusion.refs_1_, bf16[1024,2048]{1,0:T(8,128)(2,1)} %get-tuple-element.260.g.refs_0_.refs_2_.grad, ...), custom_call_target="tpu_custom_call" | custom-call | tf_op jit(solution)/shard_map/pallas_call | solution.py:269
  389.0 4.4 collective-permute-start.55
  400.5 11.5 %shard_map.291 = (bf16[512,1024]{1,0:T(8,128)(2,1)}, bf16[512,1024]{1,0:T(8,128)(2,1)}, bf16[256,1024]{1,0:T(8,128)(2,1)}, bf16[256,1024]{1,0:T(8,128)(2,1)}, bf16[256,2048]{1,0:T(8,128)(2,1)}) custom-call(s32[10]{0:T(128)} %concatenate.46.info.refs_0_, bf16[1024,2048]{1,0:T(8,128)(2,1)} %get-tuple-element.247.x.refs_0_, ...), custom_call_target="tpu_custom_call" | custom-call | tf_op jit(solution)/shard_map/pallas_call | solution.py:269
  412.7 4.8 collective-permute-done.55.refs_2_.came
  428.5 3.8 shard_map.293
  466.3 4.4 collective-permute-done.68
  475.8 3.9 shard_map.301
  (333 shorter events, 194.7 us)
Async XLA Ops:
  4.0 26.2 %collective-permute-start = (bf16[256,2048]{1,0:T(8,128)(2,1)S(1)}, bf16[256,2048]{1,0:T(8,128)(2,1)S(1)}, u32[]{:S(2)}, u32[]{:S(2)}) collective-permute-start(bf16[256,2048]{1,0:T(8,128)(2,1)S(1)} %pad_maximum_fusion.3.refs_3_.refs_11_.refs_0_.refs_8_), channel_id=1, source_target_pairs={{0,16},{8,24},{16,0},{24,8},{1,17},{9,25},{17,1},{25,9},{2,18},{10... | collective-permute-start | bytes 3145736 | tf_op jit(solution)/shard_map/ppermute | solution.py:219
  7.0 24.6 %collective-permute-start.1 = (bf16[256,2048]{1,0:T(8,128)(2,1)S(1)}, bf16[256,2048]{1,0:T(8,128)(2,1)S(1)}, u32[]{:S(2)}, u32[]{:S(2)}) collective-permute-start(bf16[256,2048]{1,0:T(8,128)(2,1)S(1)} %pad_maximum_fusion.3.refs_3_.refs_11_.refs_0_.refs_8_), channel_id=1, source_target_pairs={{0,4},{4,0},{1,5},{5,1},{2,6},{6,2},{3,7},{7,3},{8,12},{12,8},{9,1... | collective-permute-start | bytes 3145736 | tf_op jit(solution)/shard_map/ppermute | solution.py:219
  48.4 26.4 %collective-permute-start.7 = (bf16[256,2048]{1,0:T(8,128)(2,1)}, bf16[256,2048]{1,0:T(8,128)(2,1)}, u32[]{:S(2)}, u32[]{:S(2)}) collective-permute-start(bf16[256,2048]{1,0:T(8,128)(2,1)} %refs_8_.1), channel_id=1, source_target_pairs={{0,16},{8,24},{16,0},{24,8},{1,17},{9,25},{17,1},{25,9},{2,18},{10... | collective-permute-start | bytes 3145736 | tf_op jit(solution)/shard_map/ppermute | solution.py:219
  48.9 25.8 %collective-permute-start.8 = (bf16[256,2048]{1,0:T(8,128)(2,1)}, bf16[256,2048]{1,0:T(8,128)(2,1)}, u32[]{:S(2)}, u32[]{:S(2)}) collective-permute-start(bf16[256,2048]{1,0:T(8,128)(2,1)} %refs_8_.1), channel_id=1, source_target_pairs={{0,4},{4,0},{1,5},{5,1},{2,6},{6,2},{3,7},{7,3},{8,12},{12,8},{9,1... | collective-permute-start | bytes 3145736 | tf_op jit(solution)/shard_map/ppermute | solution.py:219
  63.8 32.1 %collective-permute-start.16 = (bf16[512,1024]{1,0:T(8,128)(2,1)}, bf16[512,1024]{1,0:T(8,128)(2,1)S(1)}, u32[]{:S(2)}, u32[]{:S(2)}) collective-permute-start(bf16[512,1024]{1,0:T(8,128)(2,1)} %get-tuple-element.281.refs_6_.refs_10_), channel_id=1, source_target_pairs={{0,16},{8,24},{16,0},{24,8},{1,17},{9,25},{17,1},{25,9},{2,18},{10... | collective-permute-start | bytes 3145736 | tf_op jit(solution)/shard_map/ppermute | solution.py:219
  75.3 25.3 %collective-permute-start.15 = (bf16[256,2048]{1,0:T(8,128)(2,1)}, bf16[256,2048]{1,0:T(8,128)(2,1)S(1)}, u32[]{:S(2)}, u32[]{:S(2)}) collective-permute-start(bf16[256,2048]{1,0:T(8,128)(2,1)} %collective-permute-done.7.refs_4_.refs_10_), channel_id=1, source_target_pairs={{0,4},{4,0},{1,5},{5,1},{2,6},{6,2},{3,7},{7,3},{8,12},{12,8},{9,1... | collective-permute-start | bytes 3145736 | tf_op jit(solution)/shard_map/ppermute | solution.py:219
  100.7 25.7 %collective-permute-start.13 = (bf16[256,2048]{1,0:T(8,128)(2,1)S(1)}, bf16[256,2048]{1,0:T(8,128)(2,1)}, u32[]{:S(2)}, u32[]{:S(2)}) collective-permute-start(bf16[256,2048]{1,0:T(8,128)(2,1)S(1)} %bitcast.64), channel_id=1, source_target_pairs={{0,16},{8,24},{16,0},{24,8},{1,17},{9,25},{17,1},{25,9},{2,18},{10... | collective-permute-start | bytes 3145736 | tf_op jit(solution)/shard_map/ppermute | solution.py:219
  101.3 25.3 %collective-permute-start.14 = (bf16[256,2048]{1,0:T(8,128)(2,1)S(1)}, bf16[256,2048]{1,0:T(8,128)(2,1)}, u32[]{:S(2)}, u32[]{:S(2)}) collective-permute-start(bf16[256,2048]{1,0:T(8,128)(2,1)S(1)} %bitcast.65), channel_id=1, source_target_pairs={{0,4},{4,0},{1,5},{5,1},{2,6},{6,2},{3,7},{7,3},{8,12},{12,8},{9,1... | collective-permute-start | bytes 3145736 | tf_op jit(solution)/shard_map/ppermute | solution.py:219
  105.9 25.4 %collective-permute-start.21 = (bf16[1024,1024]{1,0:T(8,128)(2,1)}, bf16[1024,1024]{1,0:T(8,128)(2,1)S(1)}, u32[]{:S(2)}, u32[]{:S(2)}) collective-permute-start(bf16[1024,1024]{1,0:T(8,128)(2,1)} %pad_maximum_fusion.1), channel_id=1, source_target_pairs={{0,8},{8,0},{16,24},{24,16},{1,9},{9,1},{17,25},{25,17},{2,10},{10... | collective-permute-start | bytes 6291464 | tf_op jit(solution)/shard_map/ppermute | solution.py:219
  144.3 42.2 %collective-permute-start.28 = (bf16[512,1024]{1,0:T(8,128)(2,1)}, bf16[512,1024]{1,0:T(8,128)(2,1)S(1)}, u32[]{:S(2)}, u32[]{:S(2)}) collective-permute-start(bf16[512,1024]{1,0:T(8,128)(2,1)} %get-tuple-element.299.refs_6_.refs_10_), channel_id=1, source_target_pairs={{0,16},{8,24},{16,0},{24,8},{1,17},{9,25},{17,1},{25,9},{2,18},{10... | collective-permute-start | bytes 3145736 | tf_op jit(solution)/shard_map/ppermute | solution.py:219
  160.8 25.7 %collective-permute-start.27 = (bf16[256,2048]{1,0:T(8,128)(2,1)}, bf16[256,2048]{1,0:T(8,128)(2,1)S(1)}, u32[]{:S(2)}, u32[]{:S(2)}) collective-permute-start(bf16[256,2048]{1,0:T(8,128)(2,1)} %get-tuple-element.298.refs_1_), channel_id=1, source_target_pairs={{0,1},{1,0},{2,3},{3,2},{4,5},{5,4},{6,7},{7,6},{8,9},{9,8},{10,11... | collective-permute-start | bytes 3145736 | tf_op jit(solution)/shard_map/ppermute | solution.py:219
  190.0 31.6 %collective-permute-start.32 = (bf16[1024,2048]{1,0:T(8,128)(2,1)}, bf16[1024,2048]{1,0:T(8,128)(2,1)}, u32[]{:S(2)}, u32[]{:S(2)}) collective-permute-start(bf16[1024,2048]{1,0:T(8,128)(2,1)} %shard_map.271), channel_id=1, source_target_pairs={{0,8},{8,0},{16,24},{24,16},{1,9},{9,1},{17,25},{25,17},{2,10},{10... | collective-permute-start | bytes 12582920 | tf_op jit(solution)/shard_map/ppermute | solution.py:219
  194.3 27.3 %collective-permute-start.31 = (bf16[512,1024]{1,0:T(8,128)(2,1)}, bf16[512,1024]{1,0:T(8,128)(2,1)}, u32[]{:S(2)}, u32[]{:S(2)}) collective-permute-start(bf16[512,1024]{1,0:T(8,128)(2,1)} %fusion.1), channel_id=1, source_target_pairs={{0,16},{8,24},{16,0},{24,8},{1,17},{9,25},{17,1},{25,9},{2,18},{10... | collective-permute-start | bytes 3145736 | tf_op jit(solution)/shard_map/ppermute | solution.py:219
  195.9 25.8 %collective-permute-start.29 = (bf16[256,2048]{1,0:T(8,128)(2,1)}, bf16[256,2048]{1,0:T(8,128)(2,1)}, u32[]{:S(2)}, u32[]{:S(2)}) collective-permute-start(bf16[256,2048]{1,0:T(8,128)(2,1)} %get-tuple-element.305.refs_1_), channel_id=1, source_target_pairs={{0,1},{1,0},{2,3},{3,2},{4,5},{5,4},{6,7},{7,6},{8,9},{9,8},{10,11... | collective-permute-start | bytes 3145736 | tf_op jit(solution)/shard_map/ppermute | solution.py:219
  225.4 28.5 %collective-permute-start.36 = (bf16[2,512,1024]{2,1,0:T(8,128)(2,1)}, bf16[2,512,1024]{2,1,0:T(8,128)(2,1)S(1)}, u32[]{:S(2)}, u32[]{:S(2)}) collective-permute-start(bf16[2,512,1024]{2,1,0:T(8,128)(2,1)} %get-tuple-element.325), channel_id=1, source_target_pairs={{0,8},{8,0},{16,24},{24,16},{1,9},{9,1},{17,25},{25,17},{2,10},{10... | collective-permute-start | bytes 6291464 | tf_op jit(solution)/shard_map/ppermute | solution.py:219
  225.6 28.3 %collective-permute-start.34 = (bf16[256,2048]{1,0:T(8,128)(2,1)}, bf16[256,2048]{1,0:T(8,128)(2,1)}, u32[]{:S(2)}, u32[]{:S(2)}) collective-permute-start(bf16[256,2048]{1,0:T(8,128)(2,1)} %get-tuple-element.322.total), channel_id=1, source_target_pairs={{0,1},{1,0},{2,3},{3,2},{4,5},{5,4},{6,7},{7,6},{8,9},{9,8},{10,11... | collective-permute-start | bytes 3145736 | tf_op jit(solution)/shard_map/ppermute | solution.py:219
  228.7 25.1 %collective-permute-start.35 = (bf16[256,2048]{1,0:T(8,128)(2,1)}, bf16[256,2048]{1,0:T(8,128)(2,1)}, u32[]{:S(2)}, u32[]{:S(2)}) collective-permute-start(bf16[256,2048]{1,0:T(8,128)(2,1)} %get-tuple-element.323.refs_3_), channel_id=1, source_target_pairs={{1,2},{2,1},{5,6},{6,5},{9,10},{10,9},{13,14},{14,13},{17,18},{18,... | collective-permute-start | bytes 3145736 | tf_op jit(solution)/shard_map/ppermute | solution.py:700
  259.6 25.4 %collective-permute-start.39 = (bf16[512,1024]{1,0:T(8,128)(2,1)}, bf16[512,1024]{1,0:T(8,128)(2,1)S(1)}, u32[]{:S(2)}, u32[]{:S(2)}) collective-permute-start(bf16[512,1024]{1,0:T(8,128)(2,1)} %fusion), channel_id=1, source_target_pairs={{0,16},{8,24},{16,0},{24,8},{1,17},{9,25},{17,1},{25,9},{2,18},{10... | collective-permute-start | bytes 3145736 | tf_op jit(solution)/shard_map/ppermute | solution.py:219
  260.2 25.9 %collective-permute-start.37 = (bf16[256,2048]{1,0:T(8,128)(2,1)}, bf16[256,2048]{1,0:T(8,128)(2,1)S(1)}, u32[]{:S(2)}, u32[]{:S(2)}) collective-permute-start(bf16[256,2048]{1,0:T(8,128)(2,1)} %get-tuple-element.335.total), channel_id=1, source_target_pairs={{0,1},{1,0},{2,3},{3,2},{4,5},{5,4},{6,7},{7,6},{8,9},{9,8},{10,11... | collective-permute-start | bytes 3145736 | tf_op jit(solution)/shard_map/ppermute | solution.py:219
  291.7 30.7 %collective-permute-start.44 = (bf16[1024,2048]{1,0:T(8,128)(2,1)}, bf16[1024,2048]{1,0:T(8,128)(2,1)}, u32[]{:S(2)}, u32[]{:S(2)}) collective-permute-start(bf16[1024,2048]{1,0:T(8,128)(2,1)} %shard_map.280), channel_id=1, source_target_pairs={{0,8},{8,0},{16,24},{24,16},{1,9},{9,1},{17,25},{25,17},{2,10},{10... | collective-permute-start | bytes 12582920 | tf_op jit(solution)/shard_map/ppermute | solution.py:219
  291.7 30.6 %collective-permute-start.43 = (bf16[512,1024]{1,0:T(8,128)(2,1)}, bf16[512,1024]{1,0:T(8,128)(2,1)S(1)}, u32[]{:S(2)}, u32[]{:S(2)}) collective-permute-start(bf16[512,1024]{1,0:T(8,128)(2,1)} %get-tuple-element.352), channel_id=1, source_target_pairs={{0,4},{4,0},{1,5},{5,1},{2,6},{6,2},{3,7},{7,3},{8,12},{12,8},{9,1... | collective-permute-start | bytes 3145736 | tf_op jit(solution)/shard_map/ppermute | solution.py:219
  293.3 29.0 %collective-permute-start.42 = (bf16[512,1024]{1,0:T(8,128)(2,1)}, bf16[512,1024]{1,0:T(8,128)(2,1)S(1)}, u32[]{:S(2)}, u32[]{:S(2)}) collective-permute-start(bf16[512,1024]{1,0:T(8,128)(2,1)} %get-tuple-element.350), channel_id=1, source_target_pairs={{0,16},{8,24},{16,0},{24,8},{1,17},{9,25},{17,1},{25,9},{2,18},{10... | collective-permute-start | bytes 3145736 | tf_op jit(solution)/shard_map/ppermute | solution.py:219
  294.4 27.9 %collective-permute-start.40 = (bf16[256,2048]{1,0:T(8,128)(2,1)}, bf16[256,2048]{1,0:T(8,128)(2,1)S(1)}, u32[]{:S(2)}, u32[]{:S(2)}) collective-permute-start(bf16[256,2048]{1,0:T(8,128)(2,1)} %get-tuple-element.347.total), channel_id=1, source_target_pairs={{0,1},{1,0},{2,3},{3,2},{4,5},{5,4},{6,7},{7,6},{8,9},{9,8},{10,11... | collective-permute-start | bytes 3145736 | tf_op jit(solution)/shard_map/ppermute | solution.py:219
  297.0 25.3 %collective-permute-start.41 = (bf16[256,2048]{1,0:T(8,128)(2,1)}, bf16[256,2048]{1,0:T(8,128)(2,1)}, u32[]{:S(2)}, u32[]{:S(2)}) collective-permute-start(bf16[256,2048]{1,0:T(8,128)(2,1)} %get-tuple-element.348.refs_3_), channel_id=1, source_target_pairs={{1,2},{2,1},{5,6},{6,5},{9,10},{10,9},{13,14},{14,13},{17,18},{18,... | collective-permute-start | bytes 3145736 | tf_op jit(solution)/shard_map/ppermute | solution.py:700
  327.0 27.2 %collective-permute-start.46 = (bf16[256,2048]{1,0:T(8,128)(2,1)}, bf16[256,2048]{1,0:T(8,128)(2,1)}, u32[]{:S(2)}, u32[]{:S(2)}) collective-permute-start(bf16[256,2048]{1,0:T(8,128)(2,1)} %get-tuple-element.376.refs_3_), channel_id=1, source_target_pairs={{1,2},{2,1},{5,6},{6,5},{9,10},{10,9},{13,14},{14,13},{17,18},{18,... | collective-permute-start | bytes 3145736 | tf_op jit(solution)/shard_map/ppermute | solution.py:700
  328.7 25.6 %collective-permute-start.45 = (bf16[256,2048]{1,0:T(8,128)(2,1)}, bf16[256,2048]{1,0:T(8,128)(2,1)}, u32[]{:S(2)}, u32[]{:S(2)}) collective-permute-start(bf16[256,2048]{1,0:T(8,128)(2,1)} %get-tuple-element.375.total), channel_id=1, source_target_pairs={{0,1},{1,0},{2,3},{3,2},{4,5},{5,4},{6,7},{7,6},{8,9},{9,8},{10,11... | collective-permute-start | bytes 3145736 | tf_op jit(solution)/shard_map/ppermute | solution.py:219
  357.9 25.7 %collective-permute-start.53 = (bf16[512,1024]{1,0:T(8,128)(2,1)}, bf16[512,1024]{1,0:T(8,128)(2,1)S(1)}, u32[]{:S(2)}, u32[]{:S(2)}) collective-permute-start(bf16[512,1024]{1,0:T(8,128)(2,1)} %get-tuple-element.397), channel_id=1, source_target_pairs={{0,4},{4,0},{1,5},{5,1},{2,6},{6,2},{3,7},{7,3},{8,12},{12,8},{9,1... | collective-permute-start | bytes 3145736 | tf_op jit(solution)/shard_map/ppermute | solution.py:219
  358.4 25.1 %collective-permute-start.52 = (bf16[512,1024]{1,0:T(8,128)(2,1)}, bf16[512,1024]{1,0:T(8,128)(2,1)S(1)}, u32[]{:S(2)}, u32[]{:S(2)}) collective-permute-start(bf16[512,1024]{1,0:T(8,128)(2,1)} %get-tuple-element.395), channel_id=1, source_target_pairs={{0,16},{8,24},{16,0},{24,8},{1,17},{9,25},{17,1},{25,9},{2,18},{10... | collective-permute-start | bytes 3145736 | tf_op jit(solution)/shard_map/ppermute | solution.py:219
  388.3 29.2 %collective-permute-start.56 = (bf16[256,2048]{1,0:T(8,128)(2,1)}, bf16[256,2048]{1,0:T(8,128)(2,1)S(1)}, u32[]{:S(2)}, u32[]{:S(2)}) collective-permute-start(bf16[256,2048]{1,0:T(8,128)(2,1)} %get-tuple-element.408.refs_3_), channel_id=1, source_target_pairs={{1,2},{2,1},{5,6},{6,5},{9,10},{10,9},{13,14},{14,13},{17,18},{18,... | collective-permute-start | bytes 3145736 | tf_op jit(solution)/shard_map/ppermute | solution.py:700
  389.0 28.5 %collective-permute-start.55 = (bf16[256,2048]{1,0:T(8,128)(2,1)}, bf16[256,2048]{1,0:T(8,128)(2,1)S(1)}, u32[]{:S(2)}, u32[]{:S(2)}) collective-permute-start(bf16[256,2048]{1,0:T(8,128)(2,1)} %get-tuple-element.407.total), channel_id=1, source_target_pairs={{0,1},{1,0},{2,3},{3,2},{4,5},{5,4},{6,7},{7,6},{8,9},{9,8},{10,11... | collective-permute-start | bytes 3145736 | tf_op jit(solution)/shard_map/ppermute | solution.py:219
  422.1 24.7 %collective-permute-start.64 = (bf16[512,1024]{1,0:T(8,128)(2,1)}, bf16[512,1024]{1,0:T(8,128)(2,1)S(1)}, u32[]{:S(2)}, u32[]{:S(2)}) collective-permute-start(bf16[512,1024]{1,0:T(8,128)(2,1)} %get-tuple-element.434), channel_id=1, source_target_pairs={{0,4},{4,0},{1,5},{5,1},{2,6},{6,2},{3,7},{7,3},{8,12},{12,8},{9,1... | collective-permute-start | bytes 3145736 | tf_op jit(solution)/shard_map/ppermute | solution.py:219
  453.0 26.8 %collective-permute-start.65 = (bf16[256,2048]{1,0:T(8,128)(2,1)}, bf16[256,2048]{1,0:T(8,128)(2,1)S(1)}, u32[]{:S(2)}, u32[]{:S(2)}) collective-permute-start(bf16[256,2048]{1,0:T(8,128)(2,1)} %shard_map.298.total), channel_id=1, source_target_pairs={{0,1},{1,0},{2,3},{3,2},{4,5},{5,4},{6,7},{7,6},{8,9},{9,8},{10,11... | collective-permute-start | bytes 3145736 | tf_op jit(solution)/shard_map/ppermute | solution.py:219
  (101 other events, 1139.1 us)
